TPU v7x, 128 devices: a whole 4x4x4 slice. The times are simulated.
128 devices in a mesh: seq: 32 (over y, x_hi, z), tp: 4 (over x_lo, core).
Axes of the slice: x: 4 (x_hi: 2, x_lo: 2; x = x_hi * 2 + x_lo), y: 4, z: 4, core: 2. Of those that a mesh axis runs over, the one named last changes fastest.
Arguments:
- gate_pre: bfloat16 [4096, 7168], P('seq', 'tp'), may hold values from -6 to 6
- up_pre: bfloat16 [4096, 7168], P('seq', 'tp'), may hold values from -6 to 6
- token_weight: bfloat16 [4096], P('seq'), may hold values from 0.099609375 to 1
- query_grad: float32 [7168, 4096], P('tp', 'seq'), may hold values from -6 to 6
Outputs:
- solution: float32 [7168, 4096], P('tp', 'seq')
- residual: float32 [7168, 4096], P('tp', 'seq')
All inputs are finite; a program needn't handle non-finite values.
Results may differ from a plain program's by a relative error of at most 0.0082.
Values may be sent and summed in bfloat16 or wider, within the bound.
A program may use at most 64 MiB of HBM per device.

v0:
```python
import jax
import jax.numpy as jnp
from jax import lax
from jax.sharding import PartitionSpec as P

ITERS = 2


DAMP = 1.0


def squares(residual):
    return lax.psum(jnp.sum(residual * residual), ("seq", "tp"))


def local(gate_pre, up_pre, token_weight, query_grad):
    hidden = (jax.nn.silu(gate_pre.astype(jnp.float32)) * up_pre.astype(jnp.float32)).astype(
        jnp.bfloat16
    )
    total = hidden.shape[0] * lax.axis_size("seq")
    solution = jnp.zeros_like(query_grad)
    residual = query_grad
    direction = query_grad
    norm_now = squares(residual)
    for step in range(ITERS):
        narrow = direction.astype(jnp.bfloat16)
        rows = jnp.dot(
            lax.all_gather(hidden, "seq", axis=0, tiled=True),
            narrow,
            preferred_element_type=jnp.float32,
        )
        piece_weight = (
            lax.all_gather(token_weight, "seq", axis=0, tiled=True).astype(jnp.float32) / total
        )
        image = lax.psum(rows, "tp")
        scaled = (image * piece_weight[:, None]).astype(jnp.bfloat16)
        back = jnp.einsum(
            "tf,tc->fc",
            lax.all_gather(hidden, "seq", axis=0, tiled=True),
            scaled,
            preferred_element_type=jnp.float32,
        )
        image = back + DAMP * direction
        alpha = norm_now / lax.psum(jnp.sum(direction * image), ("seq", "tp"))
        solution = solution + alpha * direction
        residual = residual - alpha * image
        if step + 1 < ITERS:
            norm_next = squares(residual)
            direction = residual + norm_next / norm_now * direction
            norm_now = norm_next
    return (solution, residual)


def solution(mesh):
    placed = (P("seq", "tp"), P("seq", "tp"), P("seq"), P("tp", "seq"))
    return jax.shard_map(
        local,
        mesh=mesh,
        in_specs=placed,
        out_specs=(P("tp", "seq"), P("tp", "seq")),
        check_vma=False,
    )
```

profile of v0, /device:TPU:1, one launch (start us, length us, event | category | flops | bytes accessed | tf_op | source)
XLA Modules:
  0.0 548.8 jit_solution(4380842572817917426)
XLA Ops:
  7.2 0.0 copy-start
  7.2 0.0 all-gather.3.cloned.1.call-start
  7.2 2.3 fusion.6
  9.5 0.0 all-gather.3.cloned.1.call-update
  9.5 0.0 all-reduce.4.cloned.1.call-start
  9.6 148.4 %all-gather.3.cloned.1.call-done = bf16[4096,1792]{1,0:T(8,128)(2,1)} async-done(((bf16[128,1792]{1,0:T(8,128)(2,1)}), bf16[4096,1792]{1,0:T(8,128)(2,1)}) %all-gather.3.cloned.1.call-update) | async-done | bytes 14680080 | tf_op jit(solution)/shard_map/all_gather | solution.py:39
  158.0 0.0 copy-done
  158.0 8.6 %fusion.9 = f32[4096,128]{1,0:T(8,128)} fusion(bf16[4096,1792]{1,0:T(8,128)(2,1)} %all-gather.3.cloned.1.call-done, f32[1792,128]{1,0:T(8,128)S(1)} %copy-done), kind=kOutput, calls=%fused_computation.23 | convolution fusion | flops 1879277568 | bytes 17694720 | tf_op jit(solution)/shard_map/dot_general | solution.py:27
  166.6 0.0 copy-start.1
  166.6 0.0 all-reduce.4.cloned.1.call-update
  166.6 0.0 all-reduce.6.cloned.1.call-start
  166.7 0.6 copy-done.1
  167.3 76.5 %all-gather = bf16[32,1,128]{2,1,0:T(2,128)(2,1)S(1)} all-gather(bf16[1,1,128]{2,1,0:T(2,128)(2,1)S(1)} %bitcast.8), channel_id=1, replica_groups=mesh['seq'=32,'tp'=4] {'seq'}, dimensions={0}, use_global_device_ids=true | all-gather | bytes 8448 | tf_op jit(solution)/shard_map/all_gather | solution.py:33
  243.8 0.0 all-reduce.4.cloned.1.call-done
  243.8 9.9 %multiply_reduce_fusion.2 = (f32[]{:T(128)}, f32[]{:T(128)}, f32[1792,128]{1,0:T(8,128)S(1)}) fusion(f32[1792,128]{1,0:T(8,128)S(1)} %copy-done, bf16[4096,1792]{1,0:T(8,128)(2,1)} %all-gather.3.cloned.1.call-done, f32[4096,128]{1,0:T(8,128)} %all-reduce.4.cloned.1.call-done, f32[4096]{0:T(1024)S(1)} %bitcast.6), kind=kOutput, calls=%fused_computation.18 | convolution fusion | flops 1881243648 | bytes 18628616 | tf_op jit(solution)/shard_map/tf,tc->fc/dot_general | solution.py:37
  253.7 76.5 %all-reduce = (f32[]{:T(128)}, f32[]{:T(128)}) all-reduce(f32[]{:T(128)} %get-tuple-element.3, f32[]{:T(128)} %get-tuple-element.2), channel_id=1, replica_groups=mesh['seq'=32,'tp'=4] {'seq','tp'}, use_global_device_ids=true, to_apply=%region_1.2 | all-reduce | flops 2 | bytes 16 | tf_op jit(solution)/shard_map/psum | solution.py:13
  331.6 0.8 multiply_reduce_fusion.1
  332.4 63.8 %psum.45 = f32[]{:T(128)} all-reduce(f32[]{:T(128)} %multiply_reduce_fusion.1), channel_id=1, replica_groups=mesh['seq'=32,'tp'=4] {'seq','tp'}, use_global_device_ids=true, to_apply=%region_6.7 | all-reduce | flops 1 | bytes 8 | tf_op jit(solution)/shard_map/psum | solution.py:13
  397.5 0.1 multiply_add_fusion.1
  397.6 8.6 %fusion.7 = f32[4096,128]{1,0:T(8,128)} fusion(bf16[4096,1792]{1,0:T(8,128)(2,1)} %all-gather.3.cloned.1.call-done, f32[1792,128]{1,0:T(8,128)S(1)} %multiply_add_fusion.1), kind=kOutput, calls=%fused_computation.21 | convolution fusion | flops 1879277568 | bytes 17694720 | tf_op jit(solution)/shard_map/dot_general | solution.py:27
  406.3 0.0 all-reduce.6.cloned.1.call-update
  406.3 54.2 %all-reduce.6.cloned.1.call-done = f32[4096,128]{1,0:T(8,128)} async-done(((f32[4096,128]{1,0:T(8,128)}), f32[4096,128]{1,0:T(8,128)}) %all-reduce.6.cloned.1.call-update) | async-done | bytes 2097168 | tf_op jit(solution)/shard_map/psum | solution.py:35
  460.5 12.0 %multiply_reduce_fusion = (f32[]{:T(128)}, f32[1792,128]{1,0:T(8,128)}) fusion(f32[1792,128]{1,0:T(8,128)S(1)} %multiply_add_fusion.1, bf16[4096,1792]{1,0:T(8,128)(2,1)} %all-gather.3.cloned.1.call-done, f32[4096,128]{1,0:T(8,128)} %all-reduce.6.cloned.1.call-done, f32[4096]{0:T(1024)S(1)} %bitcast.7), kind=kOutput, calls=%fused_computation.14 | convolution fusion | flops 1880784896 | bytes 18628612 | tf_op jit(solution)/shard_map/tf,tc->fc/dot_general | solution.py:37
  472.5 65.8 %psum.47 = f32[]{:T(128)} all-reduce(f32[]{:T(128)} %get-tuple-element.9), channel_id=1, replica_groups=mesh['seq'=32,'tp'=4] {'seq','tp'}, use_global_device_ids=true, to_apply=%region_9.10 | all-reduce | flops 1 | bytes 8 | tf_op jit(solution)/shard_map/psum | solution.py:44
  539.6 2.6 multiply_subtract_fusion
  (1 shorter events, 0.0 us)
Async XLA Ops:
  7.2 150.8 %copy-start = (f32[1792,128]{1,0:T(8,128)S(1)}, f32[1792,128]{1,0:T(8,128)}, u32[]{:S(2)}) copy-start(f32[1792,128]{1,0:T(8,128)} %param.7) | copy-start | bytes 2752516
  7.2 150.8 %all-gather.3.cloned.1.call-start = ((), (), s32[]{:S(2)}) async-start(), calls=%async_computation | async-start | bytes 15138816 | tf_op jit(solution)/shard_map/all_gather | solution.py:39
  9.5 234.3 %all-reduce.4.cloned.1.call-start = ((), (), s32[]{:S(2)}) async-start(), calls=%async_computation.1 | async-start | bytes 4194304 | tf_op jit(solution)/shard_map/psum | solution.py:35
  166.6 0.7 copy-start.1
  166.6 293.9 %all-reduce.6.cloned.1.call-start = ((), (), s32[]{:S(2)}) async-start(), calls=%async_computation.2 | async-start | bytes 4194304 | tf_op jit(solution)/shard_map/psum | solution.py:35
Sparse Core Ops, SparseCore 0:
  11.7 146.2 all-gather.2
  166.8 56.0 all-reduce.3
  406.4 54.0 all-reduce.5
where the time goes:
time: 550 us; the launch traced here: 549 us
  blocking collectives  283 us (51%)
  waiting for transfers between devices  203 us (37%)
  matrix products  39.2 us (7%)
  between operations  17.7 us (3%)
  other arithmetic  5.88 us (1%)
    all_gather x1, waiting for transfers between devices, local(): lax.all_gather(hidden, 'seq', axis=0, tiled=True)  148 us
    psum x2, blocking collectives, squares(): return lax.psum(jnp.sum(residual * residual), ('seq', 'tp'))  140 us
    all_gather x1, blocking collectives, local(): lax.all_gather(token_weight, 'seq', axis=0, tiled=True).astype(jnp.float32)  76.5 us
    psum x1, blocking collectives, local(): alpha = norm_now / lax.psum(jnp.sum(direction * image), ('seq', 'tp'))  65.8 us
    psum x2, waiting for transfers between devices, local(): image = lax.psum(rows, 'tp')  54.2 us
    dot_general x2, matrix products, local(): jnp.einsum('tf,tc->fc', lax.all_gather(hidden, 'seq', axis=0, tiled=True)...  21.9 us
    dot_general x2, matrix products, local(): jnp.dot(lax.all_gather(hidden, 'seq', axis=0, tiled=True), narrow, prefer...  17.2 us
  transfers between devices with their start and end apart: 3, of which 2 were waited for; matrix products, arithmetic and copies ran while one was open for 0% of the time, Pallas kernels for 0%

commit v1 on v0

v1 whole, which is shorter than its diff:
```python
import jax
import jax.numpy as jnp
from jax import lax
from jax.experimental import pallas as pl
from jax.experimental.pallas import tpu as pltpu
from jax.sharding import PartitionSpec as P

DAMP = 1.0
F32, BF16 = jnp.float32, jnp.bfloat16
MESH = pl.DeviceIdType.MESH

B = 128
FQ = 1792
R = 32
UNITS = [(0, 0), (1, 0), (3, 0), (2, 0), (0, 1), (0, 3), (0, 2), (1, 1), (1, 3), (3, 1), (3, 3), (2, 1), (1, 2), (2, 3), (3, 2), (2, 2)]
SLOT = {u: i for i, u in enumerate(UNITS)}
UT = 2 * B
T = len(UNITS) * UT
GROUPS0 = [(0, 4), (4, 7), (7, 11), (11, 13), (13, 15), (15, 16)]
GROUPS1 = [(0, 2), (2, 4), (4, 6), (6, 8), (8, 10), (10, 12), (12, 14), (14, 16)]
NSEM = 192


def kernel(gate, up, tw, q, x_out, r_out, H, nblk, hl_s, hl, qv, qb, z0, zb, z1, yown, yst, rs, sT, wb, wrow, acc, sc, fin_s, fin, ssem, rsem):
    s, t = lax.axis_index("seq"), lax.axis_index("tp")
    y, xh, z = s // 8, (s // 4) % 2, s % 4
    xl, k = t // 2, t % 2
    x = xh * 2 + xl

    def dev(x, y, z, k):
        return (y * 8 + (x // 2) * 4 + z, (x % 2) * 2 + k)

    def ystep(d):
        return dev(x, (y + d) % 4, z, k)

    def zstep(d):
        return dev(x, y, (z + d) % 4, k)

    def xstep(d):
        return dev((x + d) % 4, y, z, k)

    sib = dev(x, y, z, 1 - k)
    partner = dev((x + 2) % 4, y, z, 1 - k)
    moved = k != xh

    barrier = pltpu.get_barrier_semaphore()
    peers = [sib, partner]
    for step in (xstep, ystep, zstep):
        peers += [step(1), step(2), step(3)]
    for p in peers:
        pl.semaphore_signal(barrier, inc=1, device_id=p, device_id_type=MESH)
    pl.semaphore_wait(barrier, len(peers))

    count = [0]
    sent, sent_moved = [], []

    def remote(src, dst, device, log=True):
        i = count[0]
        count[0] += 1
        cp = pltpu.make_async_remote_copy(src_ref=src, dst_ref=dst, send_sem=ssem.at[i], recv_sem=rsem.at[i], device_id=device, device_id_type=MESH)
        (sent if log else sent_moved).append(cp)
        return cp

    def push(src, dst, device):
        cp = remote(src, dst, device)
        cp.start()
        return cp

    @pl.loop(0, B // 16)
    def _(i):
        rows = pl.ds(pl.multiple_of(i * 16, 16), 16)
        g, u = gate[rows, :].astype(F32), up[rows, :].astype(F32)
        nblk[rows, :] = (g / (1.0 + jnp.exp(-g)) * u).astype(BF16)

    wb[0, 16] = jnp.broadcast_to(tw[...].astype(F32) * (1.0 / T), (8, B))

    def block(yr, zr, core=0, off=0, n=B):
        return H.at[pl.ds(SLOT[yr, zr] * UT + core * B + off, n)]

    move_h = remote(nblk, block(0, 0), partner, log=False)
    move_w = remote(wb.at[0, 16], wb.at[0, 0], partner, log=False)
    move_q = remote(hl_s, hl, partner, log=False)

    @pl.when(moved)
    def _():
        move_h.start()
        move_w.start()

    @pl.when(jnp.logical_not(moved))
    def _():
        block(0, 0)[...] = nblk[...]
        wb[0, 0] = wb[0, 16]

    for i in range(FQ // B):
        cols = slice(i * B, (i + 1) * B)
        qt = q[cols, :].T
        hi = qt.astype(BF16)
        hl_s[:B, cols] = hi
        hl_s[B:, cols] = (qt - hi.astype(F32)).astype(BF16)

    @pl.when(moved)
    def _():
        move_q.start()
        move_h.wait_recv()

    def hop(yr, zr, axis, d, off, n):
        if axis == "y":
            return push(block(yr, zr, 0, off, n), block((yr - d) % 4, zr, 0, off, n), ystep(d))
        return push(block(yr, zr, 0, off, n), block(yr, (zr - d) % 4, 0, off, n), zstep(d))

    s1 = {(a, d): hop(0, 0, a, d, 0, B) for a in "yz" for d in (1, -1)}
    relays = {}

    def relay(yr, zr):
        relays[yr, zr] = push(block(yr, zr, 0), block(yr, zr, 1), sib)

    relay(0, 0)

    @pl.when(moved)
    def _():
        move_w.wait_recv()

    wy = [push(wb.at[0, 0], wb.at[0, (4 - d) % 4], ystep(d)) for d in (1, 2, 3)]

    s1["y", 1].wait_recv()
    s2 = [hop(3, 0, "y", 1, 0, 64)]
    s3 = {}
    s3["z", 3, 1], s3["z", 3, -1] = hop(3, 0, "z", 1, 0, 64), hop(3, 0, "z", -1, 0, 64)
    s1["y", -1].wait_recv()
    s2 += [hop(1, 0, "y", -1, 64, 64)]
    s3["z", 1, 1], s3["z", 1, -1] = hop(1, 0, "z", 1, 0, 64), hop(1, 0, "z", -1, 0, 64)
    s1["z", 1].wait_recv()
    s2 += [hop(0, 3, "z", 1, 0, 64)]
    s3["y", 3, 1], s3["y", 3, -1] = hop(0, 3, "y", 1, 64, 64), hop(0, 3, "y", -1, 64, 64)
    s1["z", -1].wait_recv()
    s2 += [hop(0, 1, "z", -1, 64, 64)]
    s3["y", 1, 1], s3["y", 1, -1] = hop(0, 1, "y", 1, 64, 64), hop(0, 1, "y", -1, 64, 64)
    for u in ((1, 0), (3, 0), (0, 1), (0, 3)):
        relay(*u)

    for cp in wy:
        cp.wait_recv()
    wz = [push(wb.at[0, pl.ds(0, 4)], wb.at[0, pl.ds(4 * ((4 - d) % 4), 4)], zstep(d)) for d in (1, 2, 3)]

    @pl.when(moved)
    def _():
        move_q.wait_recv()

    @pl.when(jnp.logical_not(moved))
    def _():
        hl[...] = hl_s[...]

    for j in range(4):
        base = ((x + j) % 4) * R
        hi = hl[pl.ds(pl.multiple_of(base, R), R), :]
        lo = hl[pl.ds(pl.multiple_of(base + B, R), R), :]
        qb[j * R : (j + 1) * R, :] = hi
        qv[j * R : (j + 1) * R, :] = hi.astype(F32) + lo.astype(F32)
    z0[...] = jnp.zeros_like(z0)
    z1[...] = jnp.zeros_like(z1)
    acc[...] = jnp.zeros_like(acc)

    for cp in s2:
        cp.wait_recv()
    s3["z", 2, 1], s3["z", 2, -1] = hop(2, 0, "z", 1, 0, 64), hop(2, 0, "z", -1, 0, 64)
    s3["y", 2, 1], s3["y", 2, -1] = hop(0, 2, "y", 1, 64, 64), hop(0, 2, "y", -1, 64, 64)
    relay(2, 0)
    relay(0, 2)
    for cp in wz:
        cp.wait_recv()
    ws = push(wb.at[0, pl.ds(0, 16)], wb.at[1, pl.ds(0, 16)], sib)

    def cols_of(group):
        return group[0] * UT, (group[1] - group[0]) * UT

    def image(it, p, group):
        @pl.loop(group[0], group[1])
        def _(u):
            at = pl.ds(pl.multiple_of(u * UT, UT), UT)
            part = lax.dot_general(p[...], H[at, :], (((1,), (1,)), ((), ())), preferred_element_type=F32)
            yown[it, :, at] = part[:R]
            yst[it, :, at] = part[R:].astype(BF16)

        c, n = cols_of(group)
        out = []
        for j in (2, 1, 3):
            out.append(push(yst.at[it, pl.ds((j - 1) * R, R), pl.ds(c, n)], rs.at[it, 3 - j, :, pl.ds(c, n)], xstep(j)))
        return out

    def reduce(it, group, copies):
        for cp in copies:
            cp.wait_recv()

        @pl.loop(group[0], group[1])
        def _(u):
            at = pl.ds(pl.multiple_of(u * UT, UT), UT)
            total = yown[it, :, at] + rs[it, 0, :, at].astype(F32) + rs[it, 1, :, at].astype(F32) + rs[it, 2, :, at].astype(F32)
            scaled = (total * wrow[0:1, at]).astype(BF16)
            sT[it, pl.ds(0, R), at] = scaled
            if it:
                acc[...] += total * scaled.astype(F32)

        c, n = cols_of(group)
        out = []
        for j in (2, 1, 3):
            out.append(push(sT.at[it, pl.ds(0, R), pl.ds(c, n)], sT.at[it, pl.ds((4 - j) * R, R), pl.ds(c, n)], xstep(j)))
        return out

    def back(it, zz, group, copies):
        for cp in copies:
            cp.wait_recv()

        @pl.loop(group[0], group[1])
        def _(u):
            at = pl.ds(pl.multiple_of(u * UT, UT), UT)
            zz[...] += jnp.dot(sT[it, :, at], H[at, :], preferred_element_type=F32)

    def wait_relays(group):
        for u in range(*group):
            relays[UNITS[u]].wait_recv()

    G = GROUPS0
    wait_relays(G[0])
    a0 = image(0, qb, G[0])
    wait_relays(G[1])
    a1 = image(0, qb, G[1])
    ws.wait_recv()
    for u, (yr, zr) in enumerate(UNITS):
        for c in range(2):
            wrow[0:8, u * UT + c * B : u * UT + (c + 1) * B] = wb[c, zr * 4 + yr]

    s4 = {}

    def onward(yr, zr, axis, d):
        off = {("z", 1): 0, ("z", -1): 32, ("y", 1): 64, ("y", -1): 96}[axis, d]
        return hop(yr, zr, axis, d, off, 32)

    s3["z", 3, 1].wait_recv()
    s4["z", 3, 1] = onward(3, 3, "z", 1)
    s3["z", 3, -1].wait_recv()
    s4["z", 3, -1] = onward(3, 1, "z", -1)
    s3["z", 1, 1].wait_recv()
    s4["z", 1, 1] = onward(1, 3, "z", 1)
    s3["z", 1, -1].wait_recv()
    s4["z", 1, -1] = onward(1, 1, "z", -1)
    s3["y", 3, 1].wait_recv()
    s4["y", 3, 1] = onward(3, 3, "y", 1)
    s3["y", 3, -1].wait_recv()
    s4["y", 3, -1] = onward(1, 3, "y", -1)
    s3["y", 1, 1].wait_recv()
    s4["y", 1, 1] = onward(3, 1, "y", 1)
    s3["y", 1, -1].wait_recv()
    s4["y", 1, -1] = onward(1, 1, "y", -1)
    for u in ((1, 1), (1, 3), (3, 1), (3, 3)):
        relay(*u)
    b0 = reduce(0, G[0], a0)
    b1 = reduce(0, G[1], a1)
    s3["z", 2, 1].wait_recv()
    s4["z", 2, 1] = onward(2, 3, "z", 1)
    s3["z", 2, -1].wait_recv()
    s4["z", 2, -1] = onward(2, 1, "z", -1)
    s3["y", 2, 1].wait_recv()
    s4["y", 2, 1] = onward(3, 2, "y", 1)
    s3["y", 2, -1].wait_recv()
    s4["y", 2, -1] = onward(1, 2, "y", -1)
    wait_relays(G[2])
    a2 = image(0, qb, G[2])
    back(0, z0, G[0], b0)
    back(0, z0, G[1], b1)

    def far(axis, i):
        for d in (1, -1):
            s4[axis, i, d].wait_recv()

    far("y", 1)
    relay(2, 1)
    far("z", 1)
    relay(1, 2)
    b2 = reduce(0, G[2], a2)
    wait_relays(G[3])
    a3 = image(0, qb, G[3])
    far("y", 3)
    relay(2, 3)
    far("z", 3)
    relay(3, 2)
    back(0, z0, G[2], b2)
    b3 = reduce(0, G[3], a3)
    wait_relays(G[4])
    a4 = image(0, qb, G[4])
    far("y", 2)
    far("z", 2)
    relay(2, 2)
    wait_relays(G[5])
    a5 = image(0, qb, G[5])
    b4 = reduce(0, G[4], a4)
    back(0, z0, G[3], b3)
    b5 = reduce(0, G[5], a5)
    back(0, z0, G[4], b4)
    back(0, z0, G[5], b5)

    zb[...] = z0[...].astype(BF16)

    def total_of(v):
        return jnp.sum(jnp.sum(v, axis=0, keepdims=True), axis=1, keepdims=True)

    def spread(which, phase):
        if phase == 0:
            return [push(sc.at[which, 0, 0], sc.at[which, 0, 1], sib)]
        step = (xstep, ystep, zstep)[phase - 1]
        return [push(sc.at[which, phase, 0], sc.at[which, phase, 4 - d], step(d)) for d in (1, 2, 3)]

    def collect(which, phase, copies):
        for cp in copies:
            cp.wait_recv()
        got = sc[which, phase, 0]
        for i in range(1, 2 if phase == 0 else 4):
            got = got + sc[which, phase, i]
        sc[which, phase + 1, 0] = got

    G = GROUPS1
    N = len(G)
    a, b = {}, {}
    a[0] = image(1, zb, G[0])
    a[1] = image(1, zb, G[1])

    def moments(i, m):
        rows = pl.ds(pl.multiple_of(i * 8, 8), 8)
        qr, zr = qv[rows, :], z0[rows, :]
        return m[0] + qr * qr, m[1] + qr * zr, m[2] + zr * zr

    zero = jnp.zeros((8, FQ), F32)
    mm = lax.fori_loop(0, B // 8, moments, (zero, zero, zero))
    row = lax.broadcasted_iota(jnp.int32, (8, B), 0)
    sc[0, 0, 0] = jnp.where(row == 0, total_of(mm[0]), jnp.where(row == 1, total_of(mm[1]), total_of(mm[2])))
    c = spread(0, 0)
    a[2] = image(1, zb, G[2])
    for i in range(N):
        b[i] = reduce(1, G[i], a[i])
        if i + 3 < N:
            a[i + 3] = image(1, zb, G[i + 3])
        if i >= 2:
            back(1, z1, G[i - 2], b[i - 2])
        if i < 4:
            collect(0, i, c)
            if i < 3:
                c = spread(0, i + 1)
    sc[1, 0, 0] = jnp.broadcast_to(total_of(acc[...]), (8, B))
    c = spread(1, 0)
    back(1, z1, G[N - 2], b[N - 2])
    collect(1, 0, c)
    c = spread(1, 1)
    back(1, z1, G[N - 1], b[N - 1])
    collect(1, 1, c)
    c = spread(1, 2)
    collect(1, 2, c)
    c = spread(1, 3)
    collect(1, 3, c)

    m = sc[0, 4, 0]
    m0, m1, m2 = m[0:1, 0:1], m[1:2, 0:1], m[2:3, 0:1]
    m3 = sc[1, 4, 0][0:1, 0:1]
    al0 = m0 / (m1 + DAMP * m0)
    n1 = al0 * al0 * (m2 - m1 * m1 / m0)
    beta = n1 / m0
    cz = 1.0 - DAMP * al0 + beta
    al1 = n1 / (DAMP * (n1 + beta * beta * m0) + cz * cz * m1 - 2.0 * cz * al0 * m2 + al0 * al0 * m3)

    for j in range(4):
        base = ((x + j) % 4) * R

        @pl.loop(0, R // 16)
        def _(i):
            rows = pl.ds(pl.multiple_of(j * R + i * 16, 16), 16)
            qr, z0r, z1r = qv[rows, :], z0[rows, :], z1[rows, :]
            r1 = qr - al0 * (z0r + DAMP * qr)
            d1 = r1 + beta * qr
            xv = al0 * qr + al1 * d1
            rv = r1 - al1 * (cz * z0r - al0 * z1r + DAMP * d1)
            qv[rows, :] = xv
            z0[rows, :] = rv
            to = pl.multiple_of(base + i * 16, 16)
            fin_s[pl.ds(to, 16), :] = xv.astype(BF16)
            fin_s[pl.ds(to + B, 16), :] = rv.astype(BF16)

    move_f = remote(fin_s, fin, partner, log=False)

    @pl.when(moved)
    def _():
        move_f.start()
        move_f.wait_recv()
        for i in range(FQ // B):
            cols = slice(i * B, (i + 1) * B)
            x_out[cols, :] = fin[:B, cols].astype(F32).T
            r_out[cols, :] = fin[B:, cols].astype(F32).T
        for cp in sent_moved:
            cp.wait_send()

    @pl.when(jnp.logical_not(moved))
    def _():
        for j in range(4):
            base = pl.multiple_of(((x + j) % 4) * R, R)
            z1[pl.ds(base, R), :] = qv[j * R : (j + 1) * R, :]
        for i in range(FQ // B):
            cols = slice(i * B, (i + 1) * B)
            x_out[cols, :] = z1[:, cols].T
        for j in range(4):
            base = pl.multiple_of(((x + j) % 4) * R, R)
            z1[pl.ds(base, R), :] = z0[j * R : (j + 1) * R, :]
        for i in range(FQ // B):
            cols = slice(i * B, (i + 1) * B)
            r_out[cols, :] = z1[:, cols].T

    for cp in sent:
        cp.wait_send()


def local(gate_pre, up_pre, token_weight, query_grad):
    vmem = pl.BlockSpec(memory_space=pltpu.VMEM)
    out = jax.ShapeDtypeStruct((FQ, B), F32)
    macs = 4 * T * FQ * B
    return pl.pallas_call(
        kernel,
        out_shape=(out, out),
        in_specs=[vmem] * 4,
        out_specs=(vmem, vmem),
        scratch_shapes=[
            pltpu.VMEM((T, FQ), BF16),
            pltpu.VMEM((B, FQ), BF16),
            pltpu.VMEM((2 * B, FQ), BF16),
            pltpu.VMEM((2 * B, FQ), BF16),
            pltpu.VMEM((B, FQ), F32),
            pltpu.VMEM((B, FQ), BF16),
            pltpu.VMEM((B, FQ), F32),
            pltpu.VMEM((B, FQ), BF16),
            pltpu.VMEM((B, FQ), F32),
            pltpu.VMEM((2, R, T), F32),
            pltpu.VMEM((2, 3 * R, T), BF16),
            pltpu.VMEM((2, 3, R, T), BF16),
            pltpu.VMEM((2, B, T), BF16),
            pltpu.VMEM((2, 17, 8, B), F32),
            pltpu.VMEM((8, T), F32),
            pltpu.VMEM((R, UT), F32),
            pltpu.VMEM((2, 5, 4, 8, B), F32),
            pltpu.VMEM((2 * B, FQ), BF16),
            pltpu.VMEM((2 * B, FQ), BF16),
            pltpu.SemaphoreType.DMA((NSEM,)),
            pltpu.SemaphoreType.DMA((NSEM,)),
        ],
        compiler_params=pltpu.CompilerParams(collective_id=0, has_side_effects=True, vmem_limit_bytes=56 * 2**20),
        cost_estimate=pl.CostEstimate(flops=2 * macs, bytes_accessed=8 * FQ * B * 4, transcendentals=FQ * B),
        name="cg",
    )(gate_pre, up_pre, token_weight[None, :], query_grad)


def solution(mesh):
    placed = (P("seq", "tp"), P("seq", "tp"), P("seq"), P("tp", "seq"))
    return jax.shard_map(
        local,
        mesh=mesh,
        in_specs=placed,
        out_specs=(P("tp", "seq"), P("tp", "seq")),
        check_vma=False,
    )
```

time: 550 us -> 137 us (0.25)
  blocking collectives: 283 us -> 0 us
  waiting for transfers between devices: 203 us -> 0 us
  Pallas kernels: 0 us -> 133 us
  matrix products: 39.2 us -> 0 us
  between operations: 17.7 us -> 0.65 us
  other arithmetic: 5.88 us -> 0 us
    psum x3 -> x0, blocking collectives: 206 us -> none  [the longest x2 140 us: squares(): return lax.psum(jnp.sum(residual * residual), ('seq', 'tp'))]
    all_gather x1 -> x0, waiting for transfers between devices: 148 us -> none  [local(): lax.all_gather(hidden, 'seq', axis=0, tiled=True)]
    pallas_call x0 -> x1, Pallas kernels: none -> 133 us  [local(): pl.pallas_call(kernel, out_shape=(out, out), in_specs=[vmem] * 4, out_spe...]
    all_gather x1 -> x0, blocking collectives: 76.5 us -> none  [local(): lax.all_gather(token_weight, 'seq', axis=0, tiled=True).astype(jnp.float32)]
    psum x2 -> x0, waiting for transfers between devices: 54.2 us -> none  [local(): image = lax.psum(rows, 'tp')]
    dot_general x4 -> x0, matrix products: 39.2 us -> none  [the longest x2 21.9 us: local(): jnp.einsum('tf,tc->fc', lax.all_gather(hidden, 'seq', axis=0, tiled=True)...]
  transfers between devices with their start and end apart: 3 -> 0, of which waited for: 2 -> 0; matrix products, arithmetic and copies ran while one was open for 0% -> 0% of each run, Pallas kernels for 0% -> 0%
where the time goes in v1:
time: 137 us
  Pallas kernels  133 us (97%)
  local copies, waits for them, and re-layouts  3.17 us (2%)
    pallas_call x1, Pallas kernels, local(): pl.pallas_call(kernel, out_shape=(out, out), in_specs=[vmem] * 4, out_spe...  133 us
    unnamed x4, local copies, waits for them, and re-layouts  3.17 us

profile of v1, /device:TPU:1, one launch (start us, length us, event | category | flops | bytes accessed | tf_op | source)
XLA Modules:
  0.0 137.0 jit_solution(2052347064346150686)
XLA Ops:
  0.6 133.2 %cg.1 = (f32[1792,128]{1,0:T(8,128)}, f32[1792,128]{1,0:T(8,128)}) custom-call(bf16[128,1792]{1,0:T(8,128)(2,1)} %gate.1, bf16[128,1792]{1,0:T(8,128)(2,1)} %up.1, bf16[1,128]{1,0:T(2,128)(2,1)} %bitcast.1, f32[1792,128]{1,0:T(8,128)} %q.1), custom_call_target="tpu_custom_call" | custom-call | flops 7516192768 | bytes 7340032 | tf_op jit(solution)/shard_map/cg/pallas_call | solution.py:421
  133.8 0.0 copy-start
  133.9 2.2 %copy.8 = f32[1792,128]{1,0:T(8,128)} copy(f32[1792,128]{1,0:T(8,128)} %get-tuple-element.4) | data formatting | bytes 1835008
  136.1 0.0 copy-done
  136.1 0.9 copy.9
Async XLA Ops:
  133.8 2.3 %copy-start = (f32[1792,128]{1,0:T(8,128)S(1)}, f32[1792,128]{1,0:T(8,128)}, u32[]{:S(2)}) copy-start(f32[1792,128]{1,0:T(8,128)} %get-tuple-element.5) | copy-start | bytes 2752516

commit v2 on v1

v2 whole, which is shorter than its diff:
```python
import jax
import jax.numpy as jnp
from jax import lax
from jax.experimental import pallas as pl
from jax.experimental.pallas import tpu as pltpu
from jax.sharding import PartitionSpec as P

DAMP = 1.0
F32, BF16 = jnp.float32, jnp.bfloat16
MESH = pl.DeviceIdType.MESH

B = 128
FQ = 1792
R = 32
UNITS = [(0, 0), (1, 0), (3, 0), (0, 1), (0, 3), (2, 0), (0, 2), (3, 3), (1, 1), (3, 1), (1, 3), (2, 1), (2, 3), (1, 2), (3, 2), (2, 2)]
SLOT = {u: i for i, u in enumerate(UNITS)}
UT = 2 * B
T = len(UNITS) * UT
GROUPS0 = [(0, 1), (1, 3), (3, 5), (5, 7), (7, 9), (9, 11), (11, 13), (13, 15), (15, 16)]
GROUPS1 = [(0, 2), (2, 4), (4, 6), (6, 8), (8, 10), (10, 12), (12, 14), (14, 15), (15, 16)]
NSEM = 250


def kernel(gate, up, tw, q, x_out, r_out, H, nblk, hl_s, hl, qv, qb, z0, zb, z1, yown, yst, rs, sT, wb, wrow, acc, sc, dv, rn, d_s, d_r, r_s, r_r, ssem, rsem):
    s, t = lax.axis_index("seq"), lax.axis_index("tp")
    y, xh, z = s // 8, (s // 4) % 2, s % 4
    xl, k = t // 2, t % 2
    x = xh * 2 + xl

    def dev(x, y, z, k):
        return (y * 8 + (x // 2) * 4 + z, (x % 2) * 2 + k)

    def ystep(d):
        return dev(x, (y + d) % 4, z, k)

    def zstep(d):
        return dev(x, y, (z + d) % 4, k)

    def xstep(d):
        return dev((x + d) % 4, y, z, k)

    sib = dev(x, y, z, 1 - k)
    partner = dev((x + 2) % 4, y, z, 1 - k)
    moved = k != xh

    barrier = pltpu.get_barrier_semaphore()
    peers = [dev((x + d) % 4, y, z, c) for d in range(4) for c in (k, 1 - k)][1:]
    plane = [(dy, dz) for dy in range(4) for dz in range(4)][1:]
    peers += [dev(x, (y + dy) % 4, (z + dz) % 4, k) for dy, dz in plane]
    for p in peers:
        pl.semaphore_signal(barrier, inc=1, device_id=p, device_id_type=MESH)

    count = [0]
    sent, sent_moved = [], []

    def remote(src, dst, device, log=True):
        i = count[0]
        assert i < NSEM
        count[0] += 1
        cp = pltpu.make_async_remote_copy(src_ref=src, dst_ref=dst, send_sem=ssem.at[i], recv_sem=rsem.at[i], device_id=device, device_id_type=MESH)
        (sent if log else sent_moved).append(cp)
        return cp

    def push(src, dst, device):
        cp = remote(src, dst, device)
        cp.start()
        return cp

    def block(yr, zr, core=0, off=0, n=B):
        return H.at[pl.ds(SLOT[yr, zr] * UT + core * B + off, n)]

    wb[0, 0] = jnp.broadcast_to(tw[...].astype(F32) * (1.0 / T), (8, B))
    move_h = [remote(nblk.at[pl.ds(i * 32, 32)], block(0, 0, 0, i * 32, 32), partner, log=False) for i in range(4)]
    wy = []
    for i in range(4):

        @pl.loop(0, 2)
        def _(h):
            rows = pl.ds(pl.multiple_of(i * 32 + h * 16, 16), 16)
            g, u = gate[rows, :].astype(F32), up[rows, :].astype(F32)
            nblk[rows, :] = (g / (1.0 + jnp.exp(-g)) * u).astype(BF16)

        if i == 0:
            pl.semaphore_wait(barrier, len(peers))
            wy += [push(wb.at[0, 0], wb.at[0, (4 - dz) % 4 * 4 + (4 - dy) % 4], dev(x, (y + dy) % 4, (z + dz) % 4, k)) for dy, dz in plane]

        @pl.when(moved)
        def _():
            move_h[i].start()

        @pl.when(jnp.logical_not(moved))
        def _():
            block(0, 0, 0, i * 32, 32)[...] = nblk[i * 32 : (i + 1) * 32]

    def hop(yr, zr, axis, d, off, n):
        if axis == "y":
            return push(block(yr, zr, 0, off, n), block((yr - d) % 4, zr, 0, off, n), ystep(d))
        return push(block(yr, zr, 0, off, n), block(yr, (zr - d) % 4, 0, off, n), zstep(d))

    sides = [("y", 1), ("z", 1), ("y", -1), ("z", -1)]
    s1 = {}
    for i in range(4):

        @pl.when(moved)
        def _():
            move_h[i].wait_recv()

        for a, d in sides:
            s1[a, d, i] = hop(0, 0, a, d, i * 32, 32)
    relays = {}

    def relay(yr, zr):
        relays[yr, zr] = push(block(yr, zr, 0), block(yr, zr, 1), sib)

    relay(0, 0)

    for i in range(FQ // B):
        cols = slice(i * B, (i + 1) * B)
        hl_s[:, cols] = q[cols, :].T.astype(BF16)
    move_q = [remote(hl_s.at[pl.ds(i * 32, 32)], hl.at[pl.ds(i * 32, 32)], partner, log=False) for i in range(4)]

    @pl.when(moved)
    def _():
        for cp in move_q:
            cp.start()

    def s1_here(a, d, half):
        s1[a, d, 2 * half].wait_recv()
        s1[a, d, 2 * half + 1].wait_recv()

    s1_here("y", 1, 0)
    s2 = [hop(3, 0, "y", 1, 0, 64)]
    s1_here("z", 1, 0)
    s2 += [hop(0, 3, "z", 1, 0, 64)]
    s1_here("y", -1, 0)
    s1_here("y", -1, 1)
    relay(1, 0)
    s2 += [hop(1, 0, "y", -1, 64, 64)]
    s1_here("z", -1, 0)
    s1_here("z", -1, 1)
    relay(0, 1)
    s2 += [hop(0, 1, "z", -1, 64, 64)]
    s1_here("y", 1, 1)
    relay(3, 0)
    s1_here("z", 1, 1)
    relay(0, 3)
    corners = [(3, 0, "z", 1), (1, 0, "z", -1), (0, 1, "y", 1), (0, 3, "y", -1)]
    s3 = [hop(*c, 64, 64) for c in corners]
    s3 += [hop(*c, 0, 64) for c in corners]
    for cp in wy:
        cp.wait_recv()
    wp = push(wb.at[0], wb.at[1], partner)

    @pl.when(moved)
    def _():
        for cp in move_q:
            cp.wait_recv()

    @pl.when(jnp.logical_not(moved))
    def _():
        hl[...] = hl_s[...]

    bases = [pl.multiple_of(((x + j) % 4) * R, R) for j in range(4)]
    for j in range(4):
        qb[j * R : (j + 1) * R, :] = hl[pl.ds(bases[j], R), :]
    z0[...] = jnp.zeros_like(z0)
    z1[...] = jnp.zeros_like(z1)
    acc[...] = jnp.zeros_like(acc)

    def cols_of(group):
        return group[0] * UT, (group[1] - group[0]) * UT

    def image(it, p, group):
        c, n = cols_of(group)
        at = pl.ds(c, n)
        part = lax.dot_general(p[...], H[at, :], (((1,), (1,)), ((), ())), preferred_element_type=F32)
        yown[it, :, at] = part[:R]
        yst[it, :, at] = part[R:].astype(BF16)
        out = []
        for j in (2, 1, 3):
            out.append(push(yst.at[it, pl.ds((j - 1) * R, R), pl.ds(c, n)], rs.at[it, 3 - j, :, pl.ds(c, n)], xstep(j)))
        return out

    def reduce(it, group, copies):
        for cp in copies:
            cp.wait_recv()

        @pl.loop(group[0], group[1])
        def _(u):
            at = pl.ds(pl.multiple_of(u * UT, UT), UT)
            total = yown[it, :, at] + rs[it, 0, :, at].astype(F32) + rs[it, 1, :, at].astype(F32) + rs[it, 2, :, at].astype(F32)
            scaled = (total * wrow[0:1, at]).astype(BF16)
            sT[it, pl.ds(0, R), at] = scaled
            if it:
                acc[...] += total * scaled.astype(F32)

        c, n = cols_of(group)
        out = []
        for j in (2, 1, 3):
            out.append(push(sT.at[it, pl.ds(0, R), pl.ds(c, n)], sT.at[it, pl.ds((4 - j) * R, R), pl.ds(c, n)], xstep(j)))
        return out

    def back(it, zz, group, copies):
        for cp in copies:
            cp.wait_recv()

        at = pl.ds(*cols_of(group))
        zz[...] += jnp.dot(sT[it, :, at], H[at, :], preferred_element_type=F32)

    def wait_relays(group):
        for u in range(*group):
            relays[UNITS[u]].wait_recv()

    G = GROUPS0
    a, b = {}, {}

    def img(i):
        wait_relays(G[i])
        a[i] = image(0, qb, G[i])

    def red(i):
        b[i] = reduce(0, G[i], a[i])

    def bck(i):
        back(0, z0, G[i], b[i])

    img(0)
    img(1)
    for cp in s2:
        cp.wait_recv()
    relay(2, 0)
    relay(0, 2)
    img(2)
    wp.wait_recv()
    other = jnp.where(moved, 1, 0)
    for u, (yr, zr) in enumerate(UNITS):
        for c in range(2):
            wrow[0:8, u * UT + c * B : u * UT + (c + 1) * B] = wb[(other + c) % 2, zr * 4 + yr]
    for cp in s3[:4]:
        cp.wait_recv()
    s4 = [hop(2, 0, "z", 1, 0, 64), hop(2, 0, "z", -1, 0, 64)]
    s4 += [hop(3, 1, "y", 1, 64, 32), hop(1, 1, "y", -1, 96, 32), hop(3, 3, "y", 1, 64, 32), hop(1, 3, "y", -1, 96, 32)]
    red(0)
    img(3)
    red(1)
    for cp in s3[4:]:
        cp.wait_recv()
    for u in UNITS[7:11]:
        relay(*u)
    s5 = [hop(0, 2, "y", 1, 0, 64), hop(0, 2, "y", -1, 0, 64)]
    s5 += [hop(1, 3, "z", 1, 64, 32), hop(1, 1, "z", -1, 96, 32), hop(3, 3, "z", 1, 64, 32), hop(3, 1, "z", -1, 96, 32)]
    red(2)
    bck(0)
    for j in range(4):
        qv[j * R : (j + 1) * R, :] = qb[j * R : (j + 1) * R, :].astype(F32)
    red(3)
    img(4)
    img(5)
    bck(1)
    for cp in s4:
        cp.wait_recv()
    s6 = [hop(2, 3, "z", 1, 0, 32), hop(2, 1, "z", -1, 32, 32)]
    relay(2, 1)
    relay(2, 3)
    bck(2)
    red(4)
    img(6)
    red(5)
    for cp in s5:
        cp.wait_recv()
    s6 += [hop(3, 2, "y", 1, 64, 32), hop(1, 2, "y", -1, 96, 32)]
    relay(1, 2)
    relay(3, 2)
    bck(3)
    img(7)
    red(6)
    for cp in s6:
        cp.wait_recv()
    relay(2, 2)
    bck(4)
    img(8)
    red(7)
    bck(5)
    red(8)
    bck(6)
    bck(7)
    bck(8)

    zb[...] = z0[...].astype(BF16)

    def total_of(v):
        return jnp.sum(jnp.sum(v, axis=0, keepdims=True), axis=1, keepdims=True)

    def spread(which, phase):
        src = sc.at[which, phase, 0]
        if phase == 0:
            to = [(1, 1 - k), (2, k), (2, 1 - k), (3, 1 - k), (1, k), (3, k), (0, 1 - k)]
            at = [3, 2, 6, 1, 7, 5, 4]
            return [push(src, sc.at[which, 0, i], dev((x + d) % 4, y, z, c)) for (d, c), i in zip(to, at)]
        return [push(src, sc.at[which, 1, (4 - dy) % 4 * 4 + (4 - dz) % 4], dev(x, (y + dy) % 4, (z + dz) % 4, k)) for dy, dz in plane]

    def collect(which, phase, copies):
        for cp in copies:
            cp.wait_recv()
        got = sc[which, phase, 0]
        for i in range(1, 8 if phase == 0 else 16):
            got = got + sc[which, phase, i]
        sc[which, phase + 1, 0] = got

    G = GROUPS1
    N = len(G)
    a, b = {}, {}
    a[0] = image(1, zb, G[0])
    a[1] = image(1, zb, G[1])

    def moments(i, m):
        rows = pl.ds(pl.multiple_of(i * 8, 8), 8)
        qr, zr = qv[rows, :], z0[rows, :]
        return m[0] + qr * qr, m[1] + qr * zr, m[2] + zr * zr

    zero = jnp.zeros((8, FQ), F32)
    mm = lax.fori_loop(0, B // 8, moments, (zero, zero, zero))
    row = lax.broadcasted_iota(jnp.int32, (8, B), 0)
    sc[0, 0, 0] = jnp.where(row == 0, total_of(mm[0]), jnp.where(row == 1, total_of(mm[1]), total_of(mm[2])))
    c = spread(0, 0)
    a[2] = image(1, zb, G[2])
    move_d = [remote(d_s.at[pl.ds(i * 64, 64)], d_r.at[pl.ds(i * 64, 64)], partner, log=False) for i in range(2)]
    for i in range(N):
        b[i] = reduce(1, G[i], a[i])
        if i + 3 < N:
            a[i + 3] = image(1, zb, G[i + 3])
        if i >= 2:
            back(1, z1, G[i - 2], b[i - 2])
        if i < 2:
            collect(0, i, c)
            if i < 1:
                c = spread(0, i + 1)
        if i == 3:
            m = sc[0, 2, 0]
            m0, m1, m2 = m[0:1, 0:1], m[1:2, 0:1], m[2:3, 0:1]
            al0 = m0 / (m1 + DAMP * m0)
            n1 = al0 * al0 * (m2 - m1 * m1 / m0)
            beta = n1 / m0
            for j in range(4):
                base = bases[j]

                @pl.loop(0, R // 16)
                def _(h):
                    rows = pl.ds(pl.multiple_of(j * R + h * 16, 16), 16)
                    to = pl.ds(pl.multiple_of(base + h * 16, 16), 16)
                    qr = qv[rows, :]
                    d1 = qr - al0 * (z0[rows, :] + DAMP * qr) + beta * qr
                    dv[to, :] = d1
                    d_s[to, :] = d1.astype(BF16)

    sc[1, 0, 0] = jnp.broadcast_to(total_of(acc[...]), (8, B))
    c = spread(1, 0)

    @pl.when(moved)
    def _():
        for cp in move_d:
            cp.start()

    back(1, z1, G[N - 2], b[N - 2])

    @pl.when(jnp.logical_not(moved))
    def _():
        for i in range(FQ // B):
            cols = slice(i * B, (i + 1) * B)
            x_out[cols, :] = dv[:, cols].T

    collect(1, 0, c)
    c = spread(1, 1)
    back(1, z1, G[N - 1], b[N - 1])

    cz = 1.0 - DAMP * al0 + beta

    @pl.loop(0, B // 16)
    def _(i):
        rows = pl.ds(pl.multiple_of(i * 16, 16), 16)
        qr, z0r = qv[rows, :], z0[rows, :]
        r1 = qr - al0 * (z0r + DAMP * qr)
        z0[rows, :] = r1
        z1[rows, :] = cz * z0r - al0 * z1[rows, :] + DAMP * (r1 + beta * qr)

    m = sc[0, 1, 0]
    o0, o1, o2 = m[0:1, 0:1], m[1:2, 0:1], m[2:3, 0:1]
    o3 = sc[1, 1, 0][0:1, 0:1]
    keep = 1.0 - DAMP * al0
    top = keep * keep * o0 - 2.0 * al0 * keep * o1 + al0 * al0 * o2
    low = DAMP * (top + 2.0 * beta * (keep * o0 - al0 * o1) + beta * beta * o0) + cz * cz * o1 - 2.0 * cz * al0 * o2 + al0 * al0 * o3
    near = jnp.where((top > 0.0) & (low > 0.0), top / low, 1.0)
    near = jnp.where((near > 1e-6) & (near < 1e6), near, 1.0)
    W = 2 * B
    move_r = [remote(r_s.at[:, pl.ds(i * W, W)], r_r.at[:, pl.ds(i * W, W)], partner, log=False) for i in range(FQ // W)]

    @pl.when(moved)
    def _():
        for i in range(FQ // W):
            cols = slice(i * W, (i + 1) * W)
            for j in range(4):
                rows = slice(j * R, (j + 1) * R)
                r_s[pl.ds(bases[j], R), cols] = (z0[rows, cols] - near * z1[rows, cols]).astype(BF16)
            move_r[i].start()
        for cp in move_d:
            cp.wait_recv()
        for i in range(FQ // B):
            cols = slice(i * B, (i + 1) * B)
            x_out[cols, :] = d_r[:, cols].astype(F32).T

    collect(1, 1, c)
    m3 = sc[1, 2, 0][0:1, 0:1]
    al1 = n1 / (DAMP * (n1 + beta * beta * m0) + cz * cz * m1 - 2.0 * cz * al0 * m2 + al0 * al0 * m3)

    @pl.when(moved)
    def _():
        ratio = al1 / near
        for i in range(FQ // W):
            move_r[i].wait_recv()
            for c in range(i * 2, i * 2 + 2):
                cols = slice(c * B, (c + 1) * B)
                r_out[cols, :] = ratio * r_r[:, cols].astype(F32).T + (1.0 - ratio) * (x_out[cols, :] - beta * q[cols, :])

    @pl.when(jnp.logical_not(moved))
    def _():
        for i in range(FQ // B):
            cols = slice(i * B, (i + 1) * B)
            for j in range(4):
                rows = slice(j * R, (j + 1) * R)
                rn[pl.ds(bases[j], R), cols] = z0[rows, cols] - al1 * z1[rows, cols]
            r_out[cols, :] = rn[:, cols].T

    @pl.loop(0, FQ // B)
    def _(i):
        rows = pl.ds(pl.multiple_of(i * B, B), B)
        x_out[rows, :] = al0 * q[rows, :] + al1 * x_out[rows, :]

    @pl.when(moved)
    def _():
        for cp in sent_moved:
            cp.wait_send()

    for cp in sent:
        cp.wait_send()


def local(gate_pre, up_pre, token_weight, query_grad):
    vmem = pl.BlockSpec(memory_space=pltpu.VMEM)
    out = jax.ShapeDtypeStruct((FQ, B), F32)
    macs = 4 * T * FQ * B
    return pl.pallas_call(
        kernel,
        out_shape=(out, out),
        in_specs=[vmem] * 4,
        out_specs=(vmem, vmem),
        scratch_shapes=[
            pltpu.VMEM((T, FQ), BF16),
            pltpu.VMEM((B, FQ), BF16),
            pltpu.VMEM((B, FQ), BF16),
            pltpu.VMEM((B, FQ), BF16),
            pltpu.VMEM((B, FQ), F32),
            pltpu.VMEM((B, FQ), BF16),
            pltpu.VMEM((B, FQ), F32),
            pltpu.VMEM((B, FQ), BF16),
            pltpu.VMEM((B, FQ), F32),
            pltpu.VMEM((2, R, T), F32),
            pltpu.VMEM((2, 3 * R, T), BF16),
            pltpu.VMEM((2, 3, R, T), BF16),
            pltpu.VMEM((2, B, T), BF16),
            pltpu.VMEM((2, 16, 8, B), F32),
            pltpu.VMEM((8, T), F32),
            pltpu.VMEM((R, UT), F32),
            pltpu.VMEM((2, 3, 16, 8, B), F32),
            pltpu.VMEM((B, FQ), F32),
            pltpu.VMEM((B, FQ), F32),
            pltpu.VMEM((B, FQ), BF16),
            pltpu.VMEM((B, FQ), BF16),
            pltpu.VMEM((B, FQ), BF16),
            pltpu.VMEM((B, FQ), BF16),
            pltpu.SemaphoreType.DMA((NSEM,)),
            pltpu.SemaphoreType.DMA((NSEM,)),
        ],
        compiler_params=pltpu.CompilerParams(collective_id=0, has_side_effects=True, vmem_limit_bytes=56 * 2**20),
        cost_estimate=pl.CostEstimate(flops=2 * macs, bytes_accessed=8 * FQ * B * 4, transcendentals=FQ * B),
        name="cg",
    )(gate_pre, up_pre, token_weight[None, :], query_grad)


def solution(mesh):
    placed = (P("seq", "tp"), P("seq", "tp"), P("seq"), P("tp", "seq"))
    return jax.shard_map(
        local,
        mesh=mesh,
        in_specs=placed,
        out_specs=(P("tp", "seq"), P("tp", "seq")),
        check_vma=False,
    )
```

time: 137 us -> 114 us (0.83)
  Pallas kernels: 133 us -> 110 us
    pallas_call x1, Pallas kernels: 133 us -> 110 us  [local(): pl.pallas_call(kernel, out_shape=(out, out), in_specs=[vmem] * 4, out_spe...]
where the time goes in v2:
time: 114 us
  Pallas kernels  110 us (96%)
  local copies, waits for them, and re-layouts  3.17 us (3%)
    pallas_call x1, Pallas kernels, local(): pl.pallas_call(kernel, out_shape=(out, out), in_specs=[vmem] * 4, out_spe...  110 us
    unnamed x4, local copies, waits for them, and re-layouts  3.17 us

profile of v2, /device:TPU:1, one launch (start us, length us, event | category | flops | bytes accessed | tf_op | source)
XLA Modules:
  0.0 113.9 jit_solution(18409223992705765561)
XLA Ops:
  0.6 110.1 %cg.1 = (f32[1792,128]{1,0:T(8,128)}, f32[1792,128]{1,0:T(8,128)}) custom-call(bf16[128,1792]{1,0:T(8,128)(2,1)} %gate.1, bf16[128,1792]{1,0:T(8,128)(2,1)} %up.1, bf16[1,128]{1,0:T(2,128)(2,1)} %bitcast.1, f32[1792,128]{1,0:T(8,128)} %q.1), custom_call_target="tpu_custom_call" | custom-call | flops 7516192768 | bytes 7340032 | tf_op jit(solution)/shard_map/cg/pallas_call | solution.py:451
  110.7 0.0 copy-start
  110.8 2.2 %copy.8 = f32[1792,128]{1,0:T(8,128)} copy(f32[1792,128]{1,0:T(8,128)} %get-tuple-element.4) | data formatting | bytes 1835008
  113.0 0.0 copy-done
  113.0 0.9 copy.9
Async XLA Ops:
  110.7 2.3 %copy-start = (f32[1792,128]{1,0:T(8,128)S(1)}, f32[1792,128]{1,0:T(8,128)}, u32[]{:S(2)}) copy-start(f32[1792,128]{1,0:T(8,128)} %get-tuple-element.5) | copy-start | bytes 2752516

commit v3 on v2

v3 whole, which is shorter than its diff:
```python
import jax
import jax.numpy as jnp
from jax import lax
from jax.experimental import pallas as pl
from jax.experimental.pallas import tpu as pltpu
from jax.sharding import PartitionSpec as P

DAMP = 1.0
F32, BF16 = jnp.float32, jnp.bfloat16
MESH = pl.DeviceIdType.MESH

B = 128
FQ = 1792
R = 32
UNITS = [(0, 0), (1, 0), (3, 0), (0, 1), (0, 3), (2, 0), (0, 2), (3, 3), (1, 1), (3, 1), (1, 3), (2, 1), (2, 3), (1, 2), (3, 2), (2, 2)]
SLOT = {u: i for i, u in enumerate(UNITS)}
UT = 2 * B
T = len(UNITS) * UT
GROUPS0 = [(0, 1), (1, 3), (3, 5), (5, 7), (7, 9), (9, 11), (11, 13), (13, 15), (15, 16)]
GROUPS1 = [(0, 2), (2, 4), (4, 6), (6, 8), (8, 10), (10, 12), (12, 14), (14, 15), (15, 16)]
NSEM = 72


def kernel(gate, up, tw, q, x_out, r_out, H, nblk, hl_s, hl, qv, qb, z0, zb, z1, yown, yst, rs, sT, wb, wrow, acc, sc, dv, rn, d_s, d_r, r_s, r_r, ssem, rsem):
    s, t = lax.axis_index("seq"), lax.axis_index("tp")
    y, xh, z = s // 8, (s // 4) % 2, s % 4
    xl, k = t // 2, t % 2
    x = xh * 2 + xl

    def dev(x, y, z, k):
        return (y * 8 + (x // 2) * 4 + z, (x % 2) * 2 + k)

    def ystep(d):
        return dev(x, (y + d) % 4, z, k)

    def zstep(d):
        return dev(x, y, (z + d) % 4, k)

    def xstep(d):
        return dev((x + d) % 4, y, z, k)

    sib = dev(x, y, z, 1 - k)
    partner = dev((x + 2) % 4, y, z, 1 - k)
    moved = k != xh

    barrier = pltpu.get_barrier_semaphore()
    peers = [dev((x + d) % 4, y, z, c) for d in range(4) for c in (k, 1 - k)][1:]
    plane = [(dy, dz) for dy in range(4) for dz in range(4)][1:]
    peers += [dev(x, (y + dy) % 4, (z + dz) % 4, k) for dy, dz in plane]
    for p in peers:
        pl.semaphore_signal(barrier, inc=1, device_id=p, device_id_type=MESH)

    used = {"send": 0, "recv": 0}

    def take(kind):
        used[kind] += 1
        assert used[kind] <= NSEM
        return used[kind] - 1

    class Copies:
        def __init__(self, sends, recv=None):
            self.sends, self.recv = sends, take("recv") if recv is None else recv

        def make(self, src, dst, device):
            return pltpu.make_async_remote_copy(src_ref=src, dst_ref=dst, send_sem=ssem.at[self.sends], recv_sem=rsem.at[self.recv], device_id=device, device_id_type=MESH)

        def push(self, src, dst, device):
            self.make(src, dst, device).start()

        def wait(self, whole):
            pltpu.make_async_copy(whole, whole, rsem.at[self.recv]).wait()

    def drain(sends, whole):
        pltpu.make_async_copy(whole, whole, ssem.at[sends]).wait()

    wb[0, 0] = jnp.broadcast_to(tw[...].astype(F32) * (1.0 / T), (8, B))
    def block(yr, zr, core=0, off=0, n=B):
        return H.at[pl.ds(SLOT[yr, zr] * UT + core * B + off, n)]

    hops = take("send")

    def hop(yr, zr, axis, d, off, n, copies):
        if axis == "y":
            return copies.make(block(yr, zr, 0, off, n), block((yr - d) % 4, zr, 0, off, n), ystep(d))
        return copies.make(block(yr, zr, 0, off, n), block(yr, (zr - d) % 4, 0, off, n), zstep(d))

    h_sends = take("send")
    h_moves = [Copies(h_sends) for _ in range(4)]
    sides = [("y", 1), ("z", 1), ("y", -1), ("z", -1)]
    s1 = {(a, 1, h): Copies(hops) for a in "yz" for h in range(2)}
    s1.update({(a, -1): Copies(hops) for a in "yz"})
    w_copies = Copies(take("send"))

    def own_piece(i):
        for a, d in sides:
            hop(0, 0, a, d, i * 32, 32, s1[(a, 1, i // 2) if d == 1 else (a, -1)]).start()

    for i in range(4):

        @pl.loop(0, 2)
        def _(h):
            rows = pl.ds(pl.multiple_of(i * 32 + h * 16, 16), 16)
            g, u = gate[rows, :].astype(F32), up[rows, :].astype(F32)
            nblk[rows, :] = (g / (1.0 + jnp.exp(-g)) * u).astype(BF16)

        if i == 0:
            pl.semaphore_wait(barrier, len(peers))

        @pl.when(moved)
        def _():
            h_moves[i].push(nblk.at[pl.ds(i * 32, 32)], block(0, 0, 0, i * 32, 32), partner)

        @pl.when(jnp.logical_not(moved))
        def _():
            block(0, 0, 0, i * 32, 32)[...] = nblk[i * 32 : (i + 1) * 32]
            own_piece(i)

    for dy, dz in plane:
        w_copies.push(wb.at[0, 0], wb.at[0, (4 - dz) % 4 * 4 + (4 - dy) % 4], dev(x, (y + dy) % 4, (z + dz) % 4, k))

    @pl.when(moved)
    def _():
        for i in range(4):
            h_moves[i].wait(block(0, 0, 0, 0, 32))
            own_piece(i)

    relay_sends = take("send")
    relay_groups = [Copies(relay_sends) for _ in GROUPS0]

    def relay(yr, zr):
        g = [SLOT[yr, zr] < e for _, e in GROUPS0].index(True)
        relay_groups[g].push(block(yr, zr, 0), block(yr, zr, 1), sib)

    relay(0, 0)

    for i in range(FQ // B):
        cols = slice(i * B, (i + 1) * B)
        hl_s[:, cols] = q[cols, :].T.astype(BF16)
    q_move = Copies(take("send"))

    @pl.when(moved)
    def _():
        for i in range(4):
            q_move.push(hl_s.at[pl.ds(i * 32, 32)], hl.at[pl.ds(i * 32, 32)], partner)

    def rows_of(n):
        return H.at[pl.ds(0, n)]

    s2 = Copies(hops)
    s1["y", 1, 0].wait(rows_of(64))
    hop(3, 0, "y", 1, 0, 64, s2).start()
    s1["z", 1, 0].wait(rows_of(64))
    hop(0, 3, "z", 1, 0, 64, s2).start()
    s1["y", -1].wait(rows_of(128))
    relay(1, 0)
    hop(1, 0, "y", -1, 64, 64, s2).start()
    s1["z", -1].wait(rows_of(128))
    relay(0, 1)
    hop(0, 1, "z", -1, 64, 64, s2).start()
    s1["y", 1, 1].wait(rows_of(64))
    relay(3, 0)
    s1["z", 1, 1].wait(rows_of(64))
    relay(0, 3)
    corners = [(3, 0, "z", 1), (1, 0, "z", -1), (0, 1, "y", 1), (0, 3, "y", -1)]
    s3 = [Copies(hops), Copies(hops)]
    for c in corners:
        hop(*c, 64, 64, s3[0]).start()
    for c in corners:
        hop(*c, 0, 64, s3[1]).start()
    w_copies.wait(wb.at[0, pl.ds(1, 15)])
    w_swap = Copies(take("send"))
    w_swap.push(wb.at[0], wb.at[1], partner)

    @pl.when(moved)
    def _():
        q_move.wait(hl)

    @pl.when(jnp.logical_not(moved))
    def _():
        hl[...] = hl_s[...]

    bases = [pl.multiple_of(((x + j) % 4) * R, R) for j in range(4)]
    for j in range(4):
        qb[j * R : (j + 1) * R, :] = hl[pl.ds(bases[j], R), :]
    z0[...] = jnp.zeros_like(z0)
    z1[...] = jnp.zeros_like(z1)
    acc[...] = jnp.zeros_like(acc)

    rs_copies, ag_copies = [], []
    rs_sends, ag_sends = [take("send"), take("send")], [take("send"), take("send")]
    for it, groups in enumerate((GROUPS0, GROUPS1)):
        before = list(zip(rs_copies[0].values(), ag_copies[0].values())) if it else [(None, None)] * len(groups)
        rs_copies.append({g: Copies(rs_sends[it], a and a.recv) for g, (a, _) in zip(groups, before)})
        ag_copies.append({g: Copies(ag_sends[it], a and a.recv) for g, (_, a) in zip(groups, before)})

    def cols_of(group):
        return group[0] * UT, (group[1] - group[0]) * UT

    def image(it, p, group):
        c, n = cols_of(group)
        at = pl.ds(c, n)
        part = lax.dot_general(p[...], H[at, :], (((1,), (1,)), ((), ())), preferred_element_type=F32)
        yown[it, :, at] = part[:R]
        yst[it, :, at] = part[R:].astype(BF16)
        for j in (2, 1, 3):
            rs_copies[it][group].push(yst.at[it, pl.ds((j - 1) * R, R), at], rs.at[it, 3 - j, :, at], xstep(j))

    def reduce(it, group, between=None):
        every = pl.ds(*cols_of(group))
        rs_copies[it][group].wait(rs.at[it, :, :, every])

        @pl.loop(group[0], group[1])
        def _(u):
            at = pl.ds(pl.multiple_of(u * UT, UT), UT)
            total = yown[it, :, at] + rs[it, 0, :, at].astype(F32) + rs[it, 1, :, at].astype(F32) + rs[it, 2, :, at].astype(F32)
            scaled = (total * wrow[0:1, at]).astype(BF16)
            sT[it, pl.ds(0, R), at] = scaled
            if it:
                acc[...] += total * scaled.astype(F32)

        if between:
            between()
        for j in (2, 1, 3):
            ag_copies[it][group].push(sT.at[it, pl.ds(0, R), every], sT.at[it, pl.ds((4 - j) * R, R), every], xstep(j))

    def back(it, zz, group):
        at = pl.ds(*cols_of(group))
        ag_copies[it][group].wait(sT.at[it, pl.ds(R, 3 * R), at])
        zz[...] += jnp.dot(sT[it, :, at], H[at, :], preferred_element_type=F32)

    G = GROUPS0

    def img(i):
        lo, hi = G[i]
        relay_groups[i].wait(rows_of((hi - lo) * B))
        image(0, qb, G[i])

    def red(i):
        reduce(0, G[i])

    def bck(i):
        back(0, z0, G[i])

    img(0)
    img(1)
    s2.wait(rows_of(256))
    relay(2, 0)
    relay(0, 2)
    img(2)
    w_swap.wait(wb.at[1])
    other = jnp.where(moved, 1, 0)
    for u, (yr, zr) in enumerate(UNITS):
        for c in range(2):
            wrow[0:8, u * UT + c * B : u * UT + (c + 1) * B] = wb[(other + c) % 2, zr * 4 + yr]
    s3[0].wait(rows_of(256))
    s4, s5, s6 = Copies(hops), Copies(hops), Copies(hops)
    for c in ((2, 0, "z", 1, 0, 64), (2, 0, "z", -1, 0, 64), (3, 1, "y", 1, 64, 32), (1, 1, "y", -1, 96, 32), (3, 3, "y", 1, 64, 32), (1, 3, "y", -1, 96, 32)):
        hop(*c, s4).start()
    red(0)
    img(3)
    red(1)
    s3[1].wait(rows_of(256))
    for u in UNITS[7:11]:
        relay(*u)
    for c in ((0, 2, "y", 1, 0, 64), (0, 2, "y", -1, 0, 64), (1, 3, "z", 1, 64, 32), (1, 1, "z", -1, 96, 32), (3, 3, "z", 1, 64, 32), (3, 1, "z", -1, 96, 32)):
        hop(*c, s5).start()
    red(2)
    bck(0)
    for j in range(4):
        qv[j * R : (j + 1) * R, :] = qb[j * R : (j + 1) * R, :].astype(F32)
    red(3)
    img(4)
    img(5)
    bck(1)
    s4.wait(rows_of(256))
    hop(2, 3, "z", 1, 0, 32, s6).start()
    hop(2, 1, "z", -1, 32, 32, s6).start()
    relay(2, 1)
    relay(2, 3)
    bck(2)
    red(4)
    img(6)
    red(5)
    s5.wait(rows_of(256))
    hop(3, 2, "y", 1, 64, 32, s6).start()
    hop(1, 2, "y", -1, 96, 32, s6).start()
    relay(1, 2)
    relay(3, 2)
    bck(3)
    img(7)
    red(6)
    s6.wait(rows_of(128))
    relay(2, 2)
    bck(4)
    img(8)
    red(7)
    bck(5)
    red(8)
    bck(6)
    bck(7)
    bck(8)

    zb[...] = z0[...].astype(BF16)

    def total_of(v):
        return jnp.sum(jnp.sum(v, axis=0, keepdims=True), axis=1, keepdims=True)

    sums = {}

    def spread(which, phase):
        src, copies = sc.at[which, phase, 0], Copies(take("send"))
        sums[which, phase] = copies
        if phase == 0:
            to = [(1, 1 - k), (2, k), (2, 1 - k), (3, 1 - k), (1, k), (3, k), (0, 1 - k)]
            for (d, c), i in zip(to, [3, 2, 6, 1, 7, 5, 4]):
                copies.push(src, sc.at[which, 0, i], dev((x + d) % 4, y, z, c))
        else:
            for dy, dz in plane:
                copies.push(src, sc.at[which, 1, (4 - dy) % 4 * 4 + (4 - dz) % 4], dev(x, (y + dy) % 4, (z + dz) % 4, k))

    def collect(which, phase):
        sums[which, phase].wait(sc.at[which, phase, pl.ds(1, 7 if phase == 0 else 15)])
        got = sc[which, phase, 0]
        for i in range(1, 8 if phase == 0 else 16):
            got = got + sc[which, phase, i]
        sc[which, phase + 1, 0] = got

    G = GROUPS1
    N = len(G)
    image(1, zb, G[0])
    image(1, zb, G[1])

    def moments(i, m):
        rows = pl.ds(pl.multiple_of(i * 8, 8), 8)
        qr, zr = qv[rows, :], z0[rows, :]
        return m[0] + qr * qr, m[1] + qr * zr, m[2] + zr * zr

    zero = jnp.zeros((8, FQ), F32)
    mm = lax.fori_loop(0, B // 8, moments, (zero, zero, zero))
    row = lax.broadcasted_iota(jnp.int32, (8, B), 0)
    sc[0, 0, 0] = jnp.where(row == 0, total_of(mm[0]), jnp.where(row == 1, total_of(mm[1]), total_of(mm[2])))
    spread(0, 0)
    image(1, zb, G[2])
    d_move = Copies(take("send"))

    def ring_sum():
        sc[1, 0, 0] = jnp.broadcast_to(total_of(acc[...]), (8, B))
        spread(1, 0)

    for i in range(N):
        reduce(1, G[i], ring_sum if i == N - 1 else None)
        if i + 3 < N:
            image(1, zb, G[i + 3])
        if i >= 2:
            back(1, z1, G[i - 2])
        if i < 2:
            collect(0, i)
            if i < 1:
                spread(0, i + 1)
        if i == 3:
            m = sc[0, 2, 0]
            m0, m1, m2 = m[0:1, 0:1], m[1:2, 0:1], m[2:3, 0:1]
            al0 = m0 / (m1 + DAMP * m0)
            n1 = al0 * al0 * (m2 - m1 * m1 / m0)
            beta = n1 / m0
            for j in range(4):
                base = bases[j]

                @pl.loop(0, R // 16)
                def _(h):
                    rows = pl.ds(pl.multiple_of(j * R + h * 16, 16), 16)
                    to = pl.ds(pl.multiple_of(base + h * 16, 16), 16)
                    qr = qv[rows, :]
                    d1 = qr - al0 * (z0[rows, :] + DAMP * qr) + beta * qr
                    dv[to, :] = d1
                    d_s[to, :] = d1.astype(BF16)

    @pl.when(moved)
    def _():
        for i in range(2):
            d_move.push(d_s.at[pl.ds(i * 64, 64)], d_r.at[pl.ds(i * 64, 64)], partner)

    back(1, z1, G[N - 2])

    @pl.when(jnp.logical_not(moved))
    def _():
        for i in range(FQ // B):
            cols = slice(i * B, (i + 1) * B)
            x_out[cols, :] = dv[:, cols].T

    collect(1, 0)
    spread(1, 1)
    back(1, z1, G[N - 1])

    cz = 1.0 - DAMP * al0 + beta

    @pl.loop(0, B // 16)
    def _(i):
        rows = pl.ds(pl.multiple_of(i * 16, 16), 16)
        qr, z0r = qv[rows, :], z0[rows, :]
        r1 = qr - al0 * (z0r + DAMP * qr)
        z0[rows, :] = r1
        z1[rows, :] = cz * z0r - al0 * z1[rows, :] + DAMP * (r1 + beta * qr)

    m = sc[0, 1, 0]
    o0, o1, o2 = m[0:1, 0:1], m[1:2, 0:1], m[2:3, 0:1]
    o3 = sc[1, 1, 0][0:1, 0:1]
    keep = 1.0 - DAMP * al0
    top = keep * keep * o0 - 2.0 * al0 * keep * o1 + al0 * al0 * o2
    low = DAMP * (top + 2.0 * beta * (keep * o0 - al0 * o1) + beta * beta * o0) + cz * cz * o1 - 2.0 * cz * al0 * o2 + al0 * al0 * o3
    near = jnp.where((top > 0.0) & (low > 0.0), top / low, 1.0)
    near = jnp.where((near > 1e-6) & (near < 1e6), near, 1.0)
    W = 2 * B
    r_sends = take("send")
    r_moves = [Copies(r_sends) for _ in range(FQ // W)]

    @pl.when(moved)
    def _():
        for i in range(FQ // W):
            cols = slice(i * W, (i + 1) * W)
            for j in range(4):
                rows = slice(j * R, (j + 1) * R)
                r_s[pl.ds(bases[j], R), cols] = (z0[rows, cols] - near * z1[rows, cols]).astype(BF16)
            part = pl.ds(i * W, W)
            r_moves[i].push(r_s.at[:, part], r_r.at[:, part], partner)

    drain(hops, rows_of(1920))
    drain(relay_sends, rows_of(16 * B))
    for it in range(2):
        drain(rs_sends[it], yst.at[it])
        drain(ag_sends[it], sT.at[it, pl.ds(R, 3 * R)])
    drain(w_copies.sends, wb.at[0, pl.ds(1, 15)])
    drain(w_swap.sends, wb.at[1])
    for which, phase in sums:
        drain(sums[which, phase].sends, sc.at[which, phase, pl.ds(1, 7 if phase == 0 else 15)])

    @pl.when(jnp.logical_not(moved))
    def _():
        for i in range(FQ // B):
            cols = slice(i * B, (i + 1) * B)
            for j in range(4):
                rows = slice(j * R, (j + 1) * R)
                rn[pl.ds(bases[j], R), cols] = z0[rows, cols] - near * z1[rows, cols]
            r_out[cols, :] = rn[:, cols].T

    @pl.when(moved)
    def _():
        d_move.wait(d_r)
        for i in range(FQ // B):
            cols = slice(i * B, (i + 1) * B)
            x_out[cols, :] = d_r[:, cols].astype(F32).T

    collect(1, 1)
    m3 = sc[1, 2, 0][0:1, 0:1]
    al1 = n1 / (DAMP * (n1 + beta * beta * m0) + cz * cz * m1 - 2.0 * cz * al0 * m2 + al0 * al0 * m3)
    ratio = al1 / near

    @pl.when(jnp.logical_not(moved))
    def _():
        @pl.loop(0, FQ // B)
        def _(i):
            rows = pl.ds(pl.multiple_of(i * B, B), B)
            qr, d1 = q[rows, :], x_out[rows, :]
            r_out[rows, :] = ratio * r_out[rows, :] + (1.0 - ratio) * (d1 - beta * qr)
            x_out[rows, :] = al0 * qr + al1 * d1

    @pl.when(moved)
    def _():
        @pl.loop(0, FQ // B)
        def _(i):
            rows = pl.ds(pl.multiple_of(i * B, B), B)
            qr, d1 = q[rows, :], x_out[rows, :]
            r_out[rows, :] = (1.0 - ratio) * (d1 - beta * qr)
            x_out[rows, :] = al0 * qr + al1 * d1

        for i in range(FQ // W):
            r_moves[i].wait(r_r.at[:, pl.ds(i * W, W)])
            for c in range(i * 2, i * 2 + 2):
                cols = slice(c * B, (c + 1) * B)
                r_out[cols, :] += ratio * r_r[:, cols].astype(F32).T
        drain(h_sends, nblk)
        drain(q_move.sends, hl_s)
        drain(d_move.sends, d_s)
        drain(r_sends, r_s)


def local(gate_pre, up_pre, token_weight, query_grad):
    vmem = pl.BlockSpec(memory_space=pltpu.VMEM)
    out = jax.ShapeDtypeStruct((FQ, B), F32)
    macs = 4 * T * FQ * B
    return pl.pallas_call(
        kernel,
        out_shape=(out, out),
        in_specs=[vmem] * 4,
        out_specs=(vmem, vmem),
        scratch_shapes=[
            pltpu.VMEM((T, FQ), BF16),
            pltpu.VMEM((B, FQ), BF16),
            pltpu.VMEM((B, FQ), BF16),
            pltpu.VMEM((B, FQ), BF16),
            pltpu.VMEM((B, FQ), F32),
            pltpu.VMEM((B, FQ), BF16),
            pltpu.VMEM((B, FQ), F32),
            pltpu.VMEM((B, FQ), BF16),
            pltpu.VMEM((B, FQ), F32),
            pltpu.VMEM((2, R, T), F32),
            pltpu.VMEM((2, 3 * R, T), BF16),
            pltpu.VMEM((2, 3, R, T), BF16),
            pltpu.VMEM((2, B, T), BF16),
            pltpu.VMEM((2, 16, 8, B), F32),
            pltpu.VMEM((8, T), F32),
            pltpu.VMEM((R, UT), F32),
            pltpu.VMEM((2, 3, 16, 8, B), F32),
            pltpu.VMEM((B, FQ), F32),
            pltpu.VMEM((B, FQ), F32),
            pltpu.VMEM((B, FQ), BF16),
            pltpu.VMEM((B, FQ), BF16),
            pltpu.VMEM((B, FQ), BF16),
            pltpu.VMEM((B, FQ), BF16),
            pltpu.SemaphoreType.DMA((NSEM,)),
            pltpu.SemaphoreType.DMA((NSEM,)),
        ],
        compiler_params=pltpu.CompilerParams(collective_id=0, has_side_effects=True, vmem_limit_bytes=56 * 2**20),
        cost_estimate=pl.CostEstimate(flops=2 * macs, bytes_accessed=8 * FQ * B * 4, transcendentals=FQ * B),
        name="cg",
    )(gate_pre, up_pre, token_weight[None, :], query_grad)


def solution(mesh):
    placed = (P("seq", "tp"), P("seq", "tp"), P("seq"), P("tp", "seq"))
    return jax.shard_map(
        local,
        mesh=mesh,
        in_specs=placed,
        out_specs=(P("tp", "seq"), P("tp", "seq")),
        check_vma=False,
    )
```

time: 114 us -> 112 us (0.982)
  the two profiles are of different devices: /device:TPU:1 before, /device:TPU:83 now
where the time goes in v3:
time: 112 us
  Pallas kernels  108 us (96%)
  local copies, waits for them, and re-layouts  3.17 us (3%)
    pallas_call x1, Pallas kernels, local(): pl.pallas_call(kernel, out_shape=(out, out), in_specs=[vmem] * 4, out_spe...  108 us
    unnamed x4, local copies, waits for them, and re-layouts  3.17 us

profile of v3, /device:TPU:83, one launch (start us, length us, event | category | flops | bytes accessed | tf_op | source)
XLA Modules:
  0.0 111.8 jit_solution(16449939577274636107)
XLA Ops:
  0.6 107.9 %cg.1 = (f32[1792,128]{1,0:T(8,128)}, f32[1792,128]{1,0:T(8,128)}) custom-call(bf16[128,1792]{1,0:T(8,128)(2,1)} %gate.1, bf16[128,1792]{1,0:T(8,128)(2,1)} %up.1, bf16[1,128]{1,0:T(2,128)(2,1)} %bitcast.1, f32[1792,128]{1,0:T(8,128)} %q.1), custom_call_target="tpu_custom_call" | custom-call | flops 7516192768 | bytes 7340032 | tf_op jit(solution)/shard_map/cg/pallas_call | solution.py:491
  108.6 0.0 copy-start
  108.6 2.2 %copy.8 = f32[1792,128]{1,0:T(8,128)} copy(f32[1792,128]{1,0:T(8,128)} %get-tuple-element.4) | data formatting | bytes 1835008
  110.8 0.0 copy-done
  110.8 0.9 copy.9
Async XLA Ops:
  108.6 2.3 %copy-start = (f32[1792,128]{1,0:T(8,128)S(1)}, f32[1792,128]{1,0:T(8,128)}, u32[]{:S(2)}) copy-start(f32[1792,128]{1,0:T(8,128)} %get-tuple-element.5) | copy-start | bytes 2752516

commit v4 on v3

--- a/solution.py
+++ b/solution.py
@@ -18,10 +18,11 @@
 T = len(UNITS) * UT
 GROUPS0 = [(0, 1), (1, 3), (3, 5), (5, 7), (7, 9), (9, 11), (11, 13), (13, 15), (15, 16)]
 GROUPS1 = [(0, 2), (2, 4), (4, 6), (6, 8), (8, 10), (10, 12), (12, 14), (14, 15), (15, 16)]
-NSEM = 72
-
-
-def kernel(gate, up, tw, q, x_out, r_out, H, nblk, hl_s, hl, qv, qb, z0, zb, z1, yown, yst, rs, sT, wb, wrow, acc, sc, dv, rn, d_s, d_r, r_s, r_r, ssem, rsem):
+RELAYED = 7
+SEMS = {"send": 18, "recv": 65}
+
+
+def kernel(gate, up, tw, q, x_out, r_out, H, nblk, hl_s, hl, qv, qb, z0, zb, z1, yown, yst, rs, sT, wb, wrow, acc, sc, dv, rn, d_r, r_s, r_r, ssem, rsem):
     s, t = lax.axis_index("seq"), lax.axis_index("tp")
     y, xh, z = s // 8, (s // 4) % 2, s % 4
     xl, k = t // 2, t % 2
@@ -54,7 +55,7 @@
 
     def take(kind):
         used[kind] += 1
-        assert used[kind] <= NSEM
+        assert used[kind] <= SEMS[kind]
         return used[kind] - 1
 
     class Copies:
@@ -74,6 +75,7 @@
         pltpu.make_async_copy(whole, whole, ssem.at[sends]).wait()
 
     wb[0, 0] = jnp.broadcast_to(tw[...].astype(F32) * (1.0 / T), (8, B))
+
     def block(yr, zr, core=0, off=0, n=B):
         return H.at[pl.ds(SLOT[yr, zr] * UT + core * B + off, n)]
 
@@ -193,6 +195,8 @@
         rs_copies.append({g: Copies(rs_sends[it], a and a.recv) for g, (a, _) in zip(groups, before)})
         ag_copies.append({g: Copies(ag_sends[it], a and a.recv) for g, (_, a) in zip(groups, before)})
 
+    onward = [{}, {g: Copies(ag_sends[1]) for g in GROUPS1[:RELAYED]}]
+
     def cols_of(group):
         return group[0] * UT, (group[1] - group[0]) * UT
 
@@ -220,12 +224,21 @@
 
         if between:
             between()
-        for j in (2, 1, 3):
+        for j in (1, 3) if group in onward[it] else (2, 1, 3):
             ag_copies[it][group].push(sT.at[it, pl.ds(0, R), every], sT.at[it, pl.ds((4 - j) * R, R), every], xstep(j))
+
+    def forward(it, group):
+        at = pl.ds(*cols_of(group))
+        ag_copies[it][group].wait(sT.at[it, pl.ds(R, 2 * R), at])
+        onward[it][group].push(sT.at[it, pl.ds(3 * R, R // 2), at], sT.at[it, pl.ds(2 * R, R // 2), at], xstep(1))
+        onward[it][group].push(sT.at[it, pl.ds(R + R // 2, R // 2), at], sT.at[it, pl.ds(2 * R + R // 2, R // 2), at], xstep(3))
 
     def back(it, zz, group):
         at = pl.ds(*cols_of(group))
-        ag_copies[it][group].wait(sT.at[it, pl.ds(R, 3 * R), at])
+        if group in onward[it]:
+            onward[it][group].wait(sT.at[it, pl.ds(2 * R, R), at])
+        else:
+            ag_copies[it][group].wait(sT.at[it, pl.ds(R, 3 * R), at])
         zz[...] += jnp.dot(sT[it, :, at], H[at, :], preferred_element_type=F32)
 
     G = GROUPS0
@@ -327,8 +340,18 @@
 
     G = GROUPS1
     N = len(G)
+    z_move = Copies(take("send"))
+
+    def swap_rows(lo, hi):
+        @pl.when(moved)
+        def _():
+            for j in range(lo, hi):
+                z_move.push(zb.at[pl.ds(j * R, R)], d_r.at[pl.ds(bases[j], R)], partner)
+
     image(1, zb, G[0])
+    swap_rows(0, 1)
     image(1, zb, G[1])
+    swap_rows(1, 2)
 
     def moments(i, m):
         rows = pl.ds(pl.multiple_of(i * 8, 8), 8)
@@ -341,7 +364,9 @@
     sc[0, 0, 0] = jnp.where(row == 0, total_of(mm[0]), jnp.where(row == 1, total_of(mm[1]), total_of(mm[2])))
     spread(0, 0)
     image(1, zb, G[2])
-    d_move = Copies(take("send"))
+    swap_rows(2, 3)
+    image(1, zb, G[3])
+    swap_rows(3, 4)
 
     def ring_sum():
         sc[1, 0, 0] = jnp.broadcast_to(total_of(acc[...]), (8, B))
@@ -349,15 +374,17 @@
 
     for i in range(N):
         reduce(1, G[i], ring_sum if i == N - 1 else None)
-        if i + 3 < N:
-            image(1, zb, G[i + 3])
-        if i >= 2:
-            back(1, z1, G[i - 2])
-        if i < 2:
-            collect(0, i)
-            if i < 1:
-                spread(0, i + 1)
+        if i + 4 < N:
+            image(1, zb, G[i + 4])
+        if 2 <= i < RELAYED + 2:
+            forward(1, G[i - 2])
+        if i >= 4:
+            back(1, z1, G[i - 4])
         if i == 3:
+            collect(0, 0)
+            spread(0, 1)
+        if i == 6:
+            collect(0, 1)
             m = sc[0, 2, 0]
             m0, m1, m2 = m[0:1, 0:1], m[1:2, 0:1], m[2:3, 0:1]
             al0 = m0 / (m1 + DAMP * m0)
@@ -373,20 +400,22 @@
                     qr = qv[rows, :]
                     d1 = qr - al0 * (z0[rows, :] + DAMP * qr) + beta * qr
                     dv[to, :] = d1
-                    d_s[to, :] = d1.astype(BF16)
-
-    @pl.when(moved)
-    def _():
-        for i in range(2):
-            d_move.push(d_s.at[pl.ds(i * 64, 64)], d_r.at[pl.ds(i * 64, 64)], partner)
-
-    back(1, z1, G[N - 2])
+
+    for i in range(N - 4, N - 1):
+        back(1, z1, G[i])
 
     @pl.when(jnp.logical_not(moved))
     def _():
         for i in range(FQ // B):
             cols = slice(i * B, (i + 1) * B)
             x_out[cols, :] = dv[:, cols].T
+
+    @pl.when(moved)
+    def _():
+        z_move.wait(d_r)
+        for i in range(FQ // B):
+            cols = slice(i * B, (i + 1) * B)
+            x_out[cols, :] = (1.0 - DAMP * al0 + beta) * q[cols, :] - al0 * d_r[:, cols].astype(F32).T
 
     collect(1, 0)
     spread(1, 1)
@@ -443,13 +472,6 @@
                 rn[pl.ds(bases[j], R), cols] = z0[rows, cols] - near * z1[rows, cols]
             r_out[cols, :] = rn[:, cols].T
 
-    @pl.when(moved)
-    def _():
-        d_move.wait(d_r)
-        for i in range(FQ // B):
-            cols = slice(i * B, (i + 1) * B)
-            x_out[cols, :] = d_r[:, cols].astype(F32).T
-
     collect(1, 1)
     m3 = sc[1, 2, 0][0:1, 0:1]
     al1 = n1 / (DAMP * (n1 + beta * beta * m0) + cz * cz * m1 - 2.0 * cz * al0 * m2 + al0 * al0 * m3)
@@ -480,7 +502,7 @@
                 r_out[cols, :] += ratio * r_r[:, cols].astype(F32).T
         drain(h_sends, nblk)
         drain(q_move.sends, hl_s)
-        drain(d_move.sends, d_s)
+        drain(z_move.sends, zb)
         drain(r_sends, r_s)
 
 
@@ -516,9 +538,8 @@
             pltpu.VMEM((B, FQ), BF16),
             pltpu.VMEM((B, FQ), BF16),
             pltpu.VMEM((B, FQ), BF16),
-            pltpu.VMEM((B, FQ), BF16),
-            pltpu.SemaphoreType.DMA((NSEM,)),
-            pltpu.SemaphoreType.DMA((NSEM,)),
+            pltpu.SemaphoreType.DMA((SEMS["send"],)),
+            pltpu.SemaphoreType.DMA((SEMS["recv"],)),
         ],
         compiler_params=pltpu.CompilerParams(collective_id=0, has_side_effects=True, vmem_limit_bytes=56 * 2**20),
         cost_estimate=pl.CostEstimate(flops=2 * macs, bytes_accessed=8 * FQ * B * 4, transcendentals=FQ * B),

time: 112 us -> 110 us (0.982)
  the two profiles are of different devices: /device:TPU:83 before, /device:TPU:1 now
where the time goes in v4:
time: 110 us
  Pallas kernels  106 us (96%)
  local copies, waits for them, and re-layouts  3.17 us (3%)
    pallas_call x1, Pallas kernels, local(): pl.pallas_call(kernel, out_shape=(out, out), in_specs=[vmem] * 4, out_spe...  106 us
    unnamed x4, local copies, waits for them, and re-layouts  3.17 us

profile of v4, /device:TPU:1, one launch (start us, length us, event | category | flops | bytes accessed | tf_op | source)
XLA Modules:
  0.0 110.3 jit_solution(6171466190078656828)
XLA Ops:
  0.6 106.4 %cg.1 = (f32[1792,128]{1,0:T(8,128)}, f32[1792,128]{1,0:T(8,128)}) custom-call(bf16[128,1792]{1,0:T(8,128)(2,1)} %gate.1, bf16[128,1792]{1,0:T(8,128)(2,1)} %up.1, bf16[1,128]{1,0:T(2,128)(2,1)} %bitcast.1, f32[1792,128]{1,0:T(8,128)} %q.1), custom_call_target="tpu_custom_call" | custom-call | flops 7516192768 | bytes 7340032 | tf_op jit(solution)/shard_map/cg/pallas_call | solution.py:513
  107.1 0.0 copy-start
  107.1 2.2 %copy.8 = f32[1792,128]{1,0:T(8,128)} copy(f32[1792,128]{1,0:T(8,128)} %get-tuple-element.4) | data formatting | bytes 1835008
  109.3 0.0 copy-done
  109.3 0.9 copy.9
Async XLA Ops:
  107.1 2.3 %copy-start = (f32[1792,128]{1,0:T(8,128)S(1)}, f32[1792,128]{1,0:T(8,128)}, u32[]{:S(2)}) copy-start(f32[1792,128]{1,0:T(8,128)} %get-tuple-element.5) | copy-start | bytes 2752516

commit v5 on v4

--- a/solution.py
+++ b/solution.py
@@ -19,10 +19,10 @@
 GROUPS0 = [(0, 1), (1, 3), (3, 5), (5, 7), (7, 9), (9, 11), (11, 13), (13, 15), (15, 16)]
 GROUPS1 = [(0, 2), (2, 4), (4, 6), (6, 8), (8, 10), (10, 12), (12, 14), (14, 15), (15, 16)]
 RELAYED = 7
-SEMS = {"send": 18, "recv": 65}
-
-
-def kernel(gate, up, tw, q, x_out, r_out, H, nblk, hl_s, hl, qv, qb, z0, zb, z1, yown, yst, rs, sT, wb, wrow, acc, sc, dv, rn, d_r, r_s, r_r, ssem, rsem):
+SEMS = {"send": 18, "recv": 72}
+
+
+def kernel(gate, up, tw, q, x_out, r_out, H, nblk, hl_s, hl, qv, qb, z0, zb, z1, yown, yst, rs, ymid, yfar, sT, wb, wrow, acc, sc, dv, rn, d_r, r_s, r_r, ssem, rsem):
     s, t = lax.axis_index("seq"), lax.axis_index("tp")
     y, xh, z = s // 8, (s // 4) % 2, s % 4
     xl, k = t // 2, t % 2
@@ -196,6 +196,7 @@
         ag_copies.append({g: Copies(ag_sends[it], a and a.recv) for g, (_, a) in zip(groups, before)})
 
     onward = [{}, {g: Copies(ag_sends[1]) for g in GROUPS1[:RELAYED]}]
+    far_part = {g: Copies(rs_sends[1]) for g in GROUPS1[:RELAYED]}
 
     def cols_of(group):
         return group[0] * UT, (group[1] - group[0]) * UT
@@ -205,18 +206,39 @@
         at = pl.ds(c, n)
         part = lax.dot_general(p[...], H[at, :], (((1,), (1,)), ((), ())), preferred_element_type=F32)
         yown[it, :, at] = part[:R]
+        if group in onward[it]:
+            ymid[0, :, at] = part[R : 2 * R]
+            ymid[1, :, at] = part[3 * R :]
+            yst[it, pl.ds(R, R), at] = part[2 * R : 3 * R].astype(BF16)
+            far_part[group].push(yst.at[it, pl.ds(R, R // 2), at], yfar.at[0, :, at], xstep(1))
+            far_part[group].push(yst.at[it, pl.ds(R + R // 2, R // 2), at], yfar.at[1, :, at], xstep(3))
+            return
         yst[it, :, at] = part[R:].astype(BF16)
         for j in (2, 1, 3):
             rs_copies[it][group].push(yst.at[it, pl.ds((j - 1) * R, R), at], rs.at[it, 3 - j, :, at], xstep(j))
 
+    def middle(it, group):
+        at = pl.ds(*cols_of(group))
+        far_part[group].wait(yfar.at[:, :, at])
+        top, low = pl.ds(0, R // 2), pl.ds(R // 2, R // 2)
+        yst[it, top, at] = (ymid[0, top, at] + yfar[0, :, at].astype(F32)).astype(BF16)
+        yst[it, low, at] = ymid[0, low, at].astype(BF16)
+        yst[it, pl.ds(2 * R, R // 2), at] = ymid[1, top, at].astype(BF16)
+        yst[it, pl.ds(2 * R + R // 2, R // 2), at] = (ymid[1, low, at] + yfar[1, :, at].astype(F32)).astype(BF16)
+        for j in (1, 3):
+            rs_copies[it][group].push(yst.at[it, pl.ds((j - 1) * R, R), at], rs.at[it, 3 - j, :, at], xstep(j))
+
     def reduce(it, group, between=None):
         every = pl.ds(*cols_of(group))
-        rs_copies[it][group].wait(rs.at[it, :, :, every])
+        near_only = group in onward[it]
+        rs_copies[it][group].wait(rs.at[it, pl.ds(0, 2 if near_only else 3), :, every])
 
         @pl.loop(group[0], group[1])
         def _(u):
             at = pl.ds(pl.multiple_of(u * UT, UT), UT)
-            total = yown[it, :, at] + rs[it, 0, :, at].astype(F32) + rs[it, 1, :, at].astype(F32) + rs[it, 2, :, at].astype(F32)
+            total = yown[it, :, at] + rs[it, 0, :, at].astype(F32) + rs[it, 2, :, at].astype(F32)
+            if not near_only:
+                total = total + rs[it, 1, :, at].astype(F32)
             scaled = (total * wrow[0:1, at]).astype(BF16)
             sT[it, pl.ds(0, R), at] = scaled
             if it:
@@ -348,10 +370,10 @@
             for j in range(lo, hi):
                 z_move.push(zb.at[pl.ds(j * R, R)], d_r.at[pl.ds(bases[j], R)], partner)
 
+    swap_rows(0, 1)
     image(1, zb, G[0])
-    swap_rows(0, 1)
     image(1, zb, G[1])
-    swap_rows(1, 2)
+    swap_rows(1, 4)
 
     def moments(i, m):
         rows = pl.ds(pl.multiple_of(i * 8, 8), 8)
@@ -364,18 +386,20 @@
     sc[0, 0, 0] = jnp.where(row == 0, total_of(mm[0]), jnp.where(row == 1, total_of(mm[1]), total_of(mm[2])))
     spread(0, 0)
     image(1, zb, G[2])
-    swap_rows(2, 3)
+    middle(1, G[0])
     image(1, zb, G[3])
-    swap_rows(3, 4)
+    middle(1, G[1])
 
     def ring_sum():
         sc[1, 0, 0] = jnp.broadcast_to(total_of(acc[...]), (8, B))
         spread(1, 0)
 
     for i in range(N):
-        reduce(1, G[i], ring_sum if i == N - 1 else None)
+        if i + 2 < RELAYED:
+            middle(1, G[i + 2])
         if i + 4 < N:
             image(1, zb, G[i + 4])
+        reduce(1, G[i], ring_sum if i == N - 1 else None)
         if 2 <= i < RELAYED + 2:
             forward(1, G[i - 2])
         if i >= 4:
@@ -528,6 +552,8 @@
             pltpu.VMEM((2, R, T), F32),
             pltpu.VMEM((2, 3 * R, T), BF16),
             pltpu.VMEM((2, 3, R, T), BF16),
+            pltpu.VMEM((2, R, T), F32),
+            pltpu.VMEM((2, R // 2, T), BF16),
             pltpu.VMEM((2, B, T), BF16),
             pltpu.VMEM((2, 16, 8, B), F32),
             pltpu.VMEM((8, T), F32),

time: 110 us -> 109 us (level)
  no operation moved by 1% of the time
where the time goes in v5:
time: 109 us
  Pallas kernels  106 us (97%)
  local copies, waits for them, and re-layouts  3.17 us (3%)
    pallas_call x1, Pallas kernels, local(): pl.pallas_call(kernel, out_shape=(out, out), in_specs=[vmem] * 4, out_spe...  106 us
    unnamed x4, local copies, waits for them, and re-layouts  3.17 us

profile of v5, /device:TPU:1, one launch (start us, length us, event | category | flops | bytes accessed | tf_op | source)
XLA Modules:
  0.0 109.3 jit_solution(16191123643589185791)
XLA Ops:
  0.6 105.5 %cg.1 = (f32[1792,128]{1,0:T(8,128)}, f32[1792,128]{1,0:T(8,128)}) custom-call(bf16[128,1792]{1,0:T(8,128)(2,1)} %gate.1, bf16[128,1792]{1,0:T(8,128)(2,1)} %up.1, bf16[1,128]{1,0:T(2,128)(2,1)} %bitcast.1, f32[1792,128]{1,0:T(8,128)} %q.1), custom_call_target="tpu_custom_call" | custom-call | flops 7516192768 | bytes 7340032 | tf_op jit(solution)/shard_map/cg/pallas_call | solution.py:537
  106.2 0.0 copy-start
  106.2 2.2 %copy.8 = f32[1792,128]{1,0:T(8,128)} copy(f32[1792,128]{1,0:T(8,128)} %get-tuple-element.4) | data formatting | bytes 1835008
  108.4 0.0 copy-done
  108.4 0.9 copy.9
Async XLA Ops:
  106.2 2.3 %copy-start = (f32[1792,128]{1,0:T(8,128)S(1)}, f32[1792,128]{1,0:T(8,128)}, u32[]{:S(2)}) copy-start(f32[1792,128]{1,0:T(8,128)} %get-tuple-element.5) | copy-start | bytes 2752516

commit v6 on v5

--- a/solution.py
+++ b/solution.py
@@ -17,7 +17,7 @@
 UT = 2 * B
 T = len(UNITS) * UT
 GROUPS0 = [(0, 1), (1, 3), (3, 5), (5, 7), (7, 9), (9, 11), (11, 13), (13, 15), (15, 16)]
-GROUPS1 = [(0, 2), (2, 4), (4, 6), (6, 8), (8, 10), (10, 12), (12, 14), (14, 15), (15, 16)]
+GROUPS1 = [(0, 1), (1, 3), (3, 5), (5, 7), (7, 9), (9, 11), (11, 13), (13, 15), (15, 16)]
 RELAYED = 7
 SEMS = {"send": 18, "recv": 72}
 
@@ -300,11 +300,11 @@
     for c in ((0, 2, "y", 1, 0, 64), (0, 2, "y", -1, 0, 64), (1, 3, "z", 1, 64, 32), (1, 1, "z", -1, 96, 32), (3, 3, "z", 1, 64, 32), (3, 1, "z", -1, 96, 32)):
         hop(*c, s5).start()
     red(2)
-    bck(0)
     for j in range(4):
         qv[j * R : (j + 1) * R, :] = qb[j * R : (j + 1) * R, :].astype(F32)
     red(3)
     img(4)
+    bck(0)
     img(5)
     bck(1)
     s4.wait(rows_of(256))
@@ -322,16 +322,16 @@
     relay(1, 2)
     relay(3, 2)
     bck(3)
+    bck(4)
+    red(6)
     img(7)
-    red(6)
     s6.wait(rows_of(128))
     relay(2, 2)
-    bck(4)
+    bck(5)
     img(8)
     red(7)
-    bck(5)
+    bck(6)
     red(8)
-    bck(6)
     bck(7)
     bck(8)
 

time: 109 us -> 109 us (level)
  no operation moved by 1% of the time
where the time goes in v6:
time: 109 us
  Pallas kernels  105 us (96%)
  local copies, waits for them, and re-layouts  3.17 us (3%)
    pallas_call x1, Pallas kernels, local(): pl.pallas_call(kernel, out_shape=(out, out), in_specs=[vmem] * 4, out_spe...  105 us
    unnamed x4, local copies, waits for them, and re-layouts  3.17 us

profile of v6, /device:TPU:1, one launch (start us, length us, event | category | flops | bytes accessed | tf_op | source)
XLA Modules:
  0.0 109.2 jit_solution(12808103404597669462)
XLA Ops:
  0.6 105.4 %cg.1 = (f32[1792,128]{1,0:T(8,128)}, f32[1792,128]{1,0:T(8,128)}) custom-call(bf16[128,1792]{1,0:T(8,128)(2,1)} %gate.1, bf16[128,1792]{1,0:T(8,128)(2,1)} %up.1, bf16[1,128]{1,0:T(2,128)(2,1)} %bitcast.1, f32[1792,128]{1,0:T(8,128)} %q.1), custom_call_target="tpu_custom_call" | custom-call | flops 7516192768 | bytes 7340032 | tf_op jit(solution)/shard_map/cg/pallas_call | solution.py:537
  106.0 0.0 copy-start
  106.0 2.2 %copy.8 = f32[1792,128]{1,0:T(8,128)} copy(f32[1792,128]{1,0:T(8,128)} %get-tuple-element.4) | data formatting | bytes 1835008
  108.3 0.0 copy-done
  108.3 0.9 copy.9
Async XLA Ops:
  106.0 2.3 %copy-start = (f32[1792,128]{1,0:T(8,128)S(1)}, f32[1792,128]{1,0:T(8,128)}, u32[]{:S(2)}) copy-start(f32[1792,128]{1,0:T(8,128)} %get-tuple-element.5) | copy-start | bytes 2752516

commit v7 on v6

--- a/solution.py
+++ b/solution.py
@@ -18,8 +18,8 @@
 T = len(UNITS) * UT
 GROUPS0 = [(0, 1), (1, 3), (3, 5), (5, 7), (7, 9), (9, 11), (11, 13), (13, 15), (15, 16)]
 GROUPS1 = [(0, 1), (1, 3), (3, 5), (5, 7), (7, 9), (9, 11), (11, 13), (13, 15), (15, 16)]
-RELAYED = 7
-SEMS = {"send": 18, "recv": 72}
+RELAYED = 6
+SEMS = {"send": 18, "recv": 70}
 
 
 def kernel(gate, up, tw, q, x_out, r_out, H, nblk, hl_s, hl, qv, qb, z0, zb, z1, yown, yst, rs, ymid, yfar, sT, wb, wrow, acc, sc, dv, rn, d_r, r_s, r_r, ssem, rsem):

time: 109 us -> 110 us (level)
  no operation moved by 1% of the time
where the time goes in v7:
time: 110 us
  Pallas kernels  106 us (96%)
  local copies, waits for them, and re-layouts  3.17 us (3%)
    pallas_call x1, Pallas kernels, local(): pl.pallas_call(kernel, out_shape=(out, out), in_specs=[vmem] * 4, out_spe...  106 us
    unnamed x4, local copies, waits for them, and re-layouts  3.17 us

profile of v7, /device:TPU:1, one launch (start us, length us, event | category | flops | bytes accessed | tf_op | source)
XLA Modules:
  0.0 109.8 jit_solution(17885456035416922323)
XLA Ops:
  0.6 106.0 %cg.1 = (f32[1792,128]{1,0:T(8,128)}, f32[1792,128]{1,0:T(8,128)}) custom-call(bf16[128,1792]{1,0:T(8,128)(2,1)} %gate.1, bf16[128,1792]{1,0:T(8,128)(2,1)} %up.1, bf16[1,128]{1,0:T(2,128)(2,1)} %bitcast.1, f32[1792,128]{1,0:T(8,128)} %q.1), custom_call_target="tpu_custom_call" | custom-call | flops 7516192768 | bytes 7340032 | tf_op jit(solution)/shard_map/cg/pallas_call | solution.py:537
  106.6 0.0 copy-start
  106.6 2.2 %copy.8 = f32[1792,128]{1,0:T(8,128)} copy(f32[1792,128]{1,0:T(8,128)} %get-tuple-element.4) | data formatting | bytes 1835008
  108.9 0.0 copy-done
  108.9 0.9 copy.9
Async XLA Ops:
  106.6 2.3 %copy-start = (f32[1792,128]{1,0:T(8,128)S(1)}, f32[1792,128]{1,0:T(8,128)}, u32[]{:S(2)}) copy-start(f32[1792,128]{1,0:T(8,128)} %get-tuple-element.5) | copy-start | bytes 2752516
